TPU v7x, 256 devices: a whole 4x4x8 slice. The times are simulated.
256 devices in a mesh: rep: 32 (over z, x_hi, core), col: 8 (over y, x_lo).
Axes of the slice: x: 4 (x_hi: 2, x_lo: 2; x = x_hi * 2 + x_lo), y: 4, z: 8, core: 2. Of those that a mesh axis runs over, the one named last changes fastest.
Arguments:
- x_rows: bfloat16 [65536, 1024], P(('rep', 'col')), may hold values from -6 to 6
- grad_out: bfloat16 [65536, 12288], P('rep', 'col'), may hold values from -0.125 to 0.125
- momentum: bfloat16 [32, 1024, 12288], P('rep', None, 'col'), may hold values from -6 to 6
- band: int32 [32], replicated, may hold values from 0 to 63, as said below
Outputs:
- new_momentum: bfloat16 [32, 1024, 12288], P('rep', None, 'col')
- update: bfloat16 [1024, 12288], P(None, 'col')
Inputs may be any that keep to these rules, and one draw needn't show every extreme that they name: `band`: 32 distinct indices, all below 64; 0 and 63 are always among them.
All inputs are finite; a program needn't handle non-finite values.
Results may differ from a plain program's by a relative error of at most 0.001.
Values may be sent and summed in bfloat16 or wider, within the bound.
No kernel may reach another device: no remote copies, remote signals or barrier semaphores. Data moves between devices by JAX's collectives and lax.ppermute only.
A program may use at most 192 MiB of HBM per device.

v0:
```python
import math

import jax
import jax.numpy as jnp
from jax import lax
from jax.sharding import PartitionSpec as P

GROUP = 256


def dct_rows(band, length):
    index = band.astype(jnp.float32)[:, None]
    cells = jnp.arange(length, dtype=jnp.float32)[None, :]
    factor = jnp.where(band == 0, math.sqrt(1.0 / length), math.sqrt(2.0 / length)).astype(
        jnp.float32
    )
    return factor[:, None] * jnp.cos(math.pi * (cells + 0.5) * index / length)


def decode(coefficients, basis):
    return jnp.einsum("ibk,kn->ibn", coefficients, basis, precision=lax.Precision.HIGHEST)


def shards(x_rows, grad_out, momentum, band):
    length = GROUP
    basis = dct_rows(band, length)
    row_count = x_rows.shape[1]
    columns = grad_out.shape[1]
    grad = lax.dot_general(
        lax.all_gather(x_rows, "col", axis=0, tiled=True),
        grad_out,
        (((0,), (0,)), ((), ())),
        preferred_element_type=jnp.float32,
    )
    blended = 0.9 * momentum[0].astype(jnp.float32) + grad
    blocks = blended.reshape(row_count, columns // length, length)
    coefficients = jnp.einsum("ibn,kn->ibk", blocks, basis, precision=lax.Precision.HIGHEST)
    summed = lax.psum(coefficients, "rep")
    update = decode(summed, basis)
    decoded = decode(coefficients, basis)
    fresh = (blended - decoded.reshape(row_count, columns)).astype(jnp.bfloat16)
    return (fresh[None], update.reshape(row_count, columns).astype(jnp.bfloat16))


def solution(mesh):
    return jax.shard_map(
        shards,
        mesh=mesh,
        in_specs=(P(("rep", "col"), None), P("rep", "col"), P("rep", None, "col"), P()),
        out_specs=(P("rep", None, "col"), P(None, "col")),
        check_vma=False,
    )
```

profile of v0, /device:TPU:1, one launch (start us, length us, event | category | flops | bytes accessed | tf_op | source)
XLA Modules:
  0.0 430.3 jit_solution(10080365975576611734)
XLA Ops:
  7.2 0.0 all-gather.2.cloned.1.call-start
  7.2 0.7 all-gather.2.cloned.1.call-update
  7.9 0.7 convert_element_type.17
  8.6 0.7 compare_select_fusion
  9.2 97.4 %all-gather.2.cloned.1.call-done = bf16[2048,1024]{1,0:T(8,128)(2,1)} async-done(((bf16[256,1024]{1,0:T(8,128)(2,1)}), bf16[2048,1024]{1,0:T(8,128)(2,1)}) %all-gather.2.cloned.1.call-update) | async-done | bytes 4194320 | tf_op jit(solution)/shard_map/all_gather | solution.py:30
  106.7 12.5 %bitcast_add_fusion = f32[1024,1536]{1,0:T(8,128)} fusion(bf16[1,1024,1536]{2,1,0:T(8,128)(2,1)} %param.6, bf16[2048,1024]{1,0:T(8,128)(2,1)} %all-gather.2.cloned.1.call-done, bf16[2048,1536]{1,0:T(8,128)(2,1)} %param.5), kind=kOutput, calls=%fused_computation | convolution fusion | flops 6447169536 | bytes 19922944 | tf_op jit(solution)/shard_map/dot_general | solution.py:29
  119.1 6.5 %copy.9 = f32[1024,1536]{0,1:T(8,128)} copy(f32[1024,1536]{1,0:T(8,128)} %bitcast_add_fusion) | data formatting | bytes 12582912 | tf_op jit(solution)/shard_map/add | solution.py:35
  125.6 6.2 %fusion.4 = f32[1024,6,32]{0,2,1:T(8,128)S(1)} fusion(f32[1024,6,256]{0,2,1:T(8,128)} %bitcast.20, f32[32]{0:T(128)S(1)} %convert_element_type.17, f32[256]{0:T(256)S(1)} %add_multiply_fusion, f32[32]{0:T(128)S(1)} %compare_select_fusion), kind=kOutput, calls=%fused_computation.7 | convolution fusion | flops 604004352 | bytes 7079168 | tf_op jit(solution)/shard_map/ibn,kn->ibk/dot_general | solution.py:37
  131.8 0.0 copy-start
  131.8 8.0 %fusion.2 = f32[1024,6,256]{0,2,1:T(8,128)} fusion(f32[1024,6,32]{0,2,1:T(8,128)S(1)} %fusion.4, f32[32]{0:T(128)S(1)} %convert_element_type.17, f32[256]{0:T(256)S(1)} %add_multiply_fusion, f32[32]{0:T(128)S(1)} %compare_select_fusion), kind=kOutput, calls=%fused_computation.5 | convolution fusion | flops 604004352 | bytes 7079168 | tf_op jit(solution)/shard_map/ibk,kn->ibn/dot_general | solution.py:21
  139.8 0.0 all-reduce.2.cloned.1.call-start
  139.8 0.0 copy-done
  139.8 0.7 all-reduce.2.cloned.1.call-update
  140.5 6.6 %copy.11 = f32[1024,1536]{1,0:T(8,128)} copy(f32[1024,1536]{0,1:T(8,128)} %bitcast.19) | data formatting | bytes 12582912 | tf_op jit(solution)/shard_map/reshape | solution.py:41
  147.1 7.3 %fusion = bf16[1,1024,1536]{2,1,0:T(8,128)(2,1)} fusion(f32[1024,1536]{1,0:T(8,128)} %bitcast_add_fusion, f32[1024,1536]{1,0:T(8,128)} %copy.11), kind=kLoop, calls=%fused_computation.2 | loop fusion | flops 3145728 | bytes 15728640 | tf_op jit(solution)/shard_map/broadcast_in_dim | solution.py:42
  154.5 259.2 %all-reduce.2.cloned.1.call-done = f32[1024,6,32]{0,2,1:T(8,128)} async-done(((f32[1024,6,32]{0,2,1:T(8,128)}), f32[1024,6,32]{0,2,1:T(8,128)}) %all-reduce.2.cloned.1.call-update) | async-done | bytes 786448 | tf_op jit(solution)/shard_map/psum | solution.py:38
  413.7 6.8 %convolution_convert_fusion = bf16[1024,6,256]{0,2,1:T(8,128)(2,1)S(1)} fusion(f32[1024,6,32]{0,2,1:T(8,128)} %all-reduce.2.cloned.1.call-done, f32[32]{0:T(128)S(1)} %convert_element_type.17, f32[256]{0:T(256)S(1)} %add_multiply_fusion, f32[32]{0:T(128)S(1)} %compare_select_fusion), kind=kOutput, calls=%fused_computation.3 | convolution fusion | flops 605577216 | bytes 3933440 | tf_op jit(solution)/shard_map/ibk,kn->ibn/dot_general | solution.py:21
  420.5 2.9 copy.12
  (1 shorter events, 0.0 us)
Async XLA Ops:
  7.2 99.5 %all-gather.2.cloned.1.call-start = ((), (), s32[]{:S(2)}) async-start(), calls=%async_computation | async-start | bytes 4718592 | tf_op jit(solution)/shard_map/all_gather | solution.py:30
  131.8 8.0 %copy-start = (f32[1024,6,32]{0,2,1:T(8,128)}, f32[1024,6,32]{0,2,1:T(8,128)S(1)}, u32[]{:S(2)}) copy-start(f32[1024,6,32]{0,2,1:T(8,128)S(1)} %fusion.4) | copy-start | bytes 2359300
  139.8 273.9 %all-reduce.2.cloned.1.call-start = ((), (), s32[]{:S(2)}) async-start(), calls=%async_computation.1 | async-start | bytes 1572864 | tf_op jit(solution)/shard_map/psum | solution.py:38
Sparse Core Ops, SparseCore 0:
  9.8 96.8 all-gather.1
  143.8 269.8 all-reduce.1
where the time goes:
time: 431 us; the launch traced here: 430 us
  waiting for transfers between devices  358 us (83%)
  matrix products  33.4 us (8%)
  local copies, waits for them, and re-layouts  16 us (4%)
  between operations  14.1 us (3%)
  other arithmetic  8.67 us (2%)
    psum x1, waiting for transfers between devices, shards(): summed = lax.psum(coefficients, 'rep')  259 us
    all_gather x1, waiting for transfers between devices, shards(): lax.all_gather(x_rows, 'col', axis=0, tiled=True)  97.4 us
    dot_general x2, matrix products, decode(): jnp.einsum('ibk,kn->ibn', coefficients, basis, precision=lax.Precision.HI...  14.8 us
    dot_general x1, matrix products, shards(): lax.dot_general(lax.all_gather(x_rows, 'col', axis=0, tiled=True), grad_o...  12.5 us
  transfers between devices with their start and end apart: 2, of which 2 were waited for; matrix products, arithmetic and copies ran while one was open for 4% of the time, Pallas kernels for 0%

commit v1 on v0

v1 whole, which is shorter than its diff:
```python
import functools
import math

import jax
import jax.numpy as jnp
from jax import lax
from jax.experimental import pallas as pl
from jax.experimental.pallas import tpu as pltpu
from jax.sharding import Mesh
from jax.sharding import PartitionSpec as P

GROUP = 256
TILE = 512
F32 = jnp.float32
BF16 = jnp.bfloat16
PAIR = [(0, 1), (1, 0)]


def ring(size, step):
    return [(i, (i + step) % size) for i in range(size)]


def dct_rows(band, length):
    index = band.astype(F32)[:, None]
    cells = jnp.arange(length, dtype=F32)[None, :]
    factor = jnp.where(band == 0, math.sqrt(1.0 / length), math.sqrt(2.0 / length)).astype(F32)
    return factor[:, None] * jnp.cos(math.pi * (cells + 0.5) * index / length)


def split(value):
    high = value.astype(BF16)
    return high, (value - high.astype(F32)).astype(BF16)


def dot(a, b, dims):
    return lax.dot_general(a, b, ((dims[:1], dims[1:]), ((), ())), preferred_element_type=F32)


def decode(coefficients, stacked):
    high, low = split(coefficients)
    return dot(jnp.concatenate([high, low, high], axis=0), stacked, (0, 0))


def encode(pair, values, band):
    both = dot(pair, values, (1, 1))
    return both[:band] + both[band:]


def block(index, size):
    return slice(index * size, (index + 1) * size)


def load_kernel(band, grad_in, momentum, pair, coded, total, kept):
    blocks = total.shape[1] // GROUP
    for b in range(blocks):
        values = momentum[0, :, block(b, GROUP)]
        total[:, block(b, GROUP)] = 0.9 * values.astype(F32)
        kept[block(b, band), :] = 0.9 * encode(pair[...], values, band)
    for b in range(blocks):
        high, low = split(encode(pair[...], grad_in[:, block(b, GROUP)], band))
        coded[block(b, band), :] = high
        coded[block(blocks + b, band), :] = low


def tokens_of(place, count):
    return pl.ds(pl.multiple_of(place * count, count), count)


def chunks(groups, refs):
    taken, out = 0, []
    for count in groups:
        out.append(refs[taken : taken + count])
        taken += count
    return out, refs[taken:]


def take(pieces, columns):
    parts = [piece[:, columns] for piece in pieces]
    return parts[0] if len(parts) == 1 else jnp.concatenate(parts, axis=0)


def code_sum(places, xs, coded, columns):
    value = 0.0
    half = coded.shape[0] // 2
    for s, pieces in enumerate(xs):
        x = take(pieces, columns)
        tokens = tokens_of(places[s], x.shape[0])
        value = value + (dot(coded[:half, tokens], x, (1, 0)) + dot(coded[half:, tokens], x, (1, 0)))
    return value


def grad_sum(places, xs, grad_in, rows, columns):
    value = 0.0
    for s, pieces in enumerate(xs):
        x = take(pieces, rows)
        value = value + dot(x, grad_in[tokens_of(places[s], x.shape[0]), columns], (0, 0))
    return value


def add_kernel(groups, places, *refs):
    xs, refs = chunks(groups, refs)
    grad_in, coded, total, kept, total_out, kept_out = refs

    @pl.loop(0, total.shape[0] // TILE)
    def _(i):
        rows = pl.ds(pl.multiple_of(i * TILE, TILE), TILE)
        kept_out[:, rows] = kept[:, rows] + code_sum(places, xs, coded, rows)
        for b in range(total.shape[1] // TILE):
            columns = block(b, TILE)
            total_out[rows, columns] = total[rows, columns] + grad_sum(places, xs, grad_in, rows, columns)


def code_kernel(groups, places, core, *refs):
    xs, refs = chunks(groups, refs)
    coded, kept, kept_out, mine, other = refs
    rows = kept.shape[1] // 2

    def half(index, out):
        columns = pl.ds(pl.multiple_of(index * rows, rows), rows)
        value = kept[:, columns] + code_sum(places, xs, coded, columns)
        kept_out[:, columns] = value
        for t in range(rows // 128):
            out[block(t, value.shape[0]), :] = value[:, block(t, 128)]

    half(1 - core[0], other)
    half(core[0], mine)


def fresh_kernel(groups, band, places, *refs):
    xs, refs = chunks(groups, refs)
    grad_in, total, kept, stacked, fresh, staged, sems = refs
    steps = total.shape[0] // TILE
    for i in range(steps):
        rows = block(i, TILE)
        for b in range(total.shape[1] // GROUP):
            columns = block(b, GROUP)
            value = total[rows, columns] + grad_sum(places, xs, grad_in, rows, columns)
            value = value - decode(kept[block(b, band), rows], stacked[...])
            staged[rows, columns] = value.astype(BF16)
        pltpu.make_async_copy(staged.at[rows], fresh.at[0, rows], sems.at[i]).start()
    for i in range(steps):
        rows = block(i, TILE)
        pltpu.make_async_copy(staged.at[rows], fresh.at[0, rows], sems.at[i]).wait()


def part_kernel(chips, parts, spread):
    rows = parts.shape[0] // chips
    value = parts[:rows, :]
    for i in range(1, chips):
        value = value + parts[block(i, rows), :]
    for i in range(chips):
        spread[block(i, rows), :] = value


def update_kernel(band, core, mine, other, stacked, update):
    step = pl.program_id(0)
    kept = mine.shape[0] // 4
    value = jnp.where(step == core[0], mine[...], other[...])
    for b in range(update.shape[1] // GROUP):
        parts = [value[t * kept + b * band : t * kept + (b + 1) * band] for t in range(4)]
        update[:, block(b, GROUP)] = decode(jnp.concatenate(parts, axis=1), stacked[...]).astype(BF16)


VMEM = pl.BlockSpec(memory_space=pltpu.VMEM)
SMEM = pl.BlockSpec(memory_space=pltpu.SMEM)
ANY = pl.BlockSpec(memory_space=pl.ANY)


def params(mib):
    return pltpu.CompilerParams(vmem_limit_bytes=mib << 20)


def held(value):
    return pltpu.with_memory_space_constraint(value, pltpu.VMEM)


def estimate(flops, size):
    return pl.CostEstimate(flops=flops, bytes_accessed=size, transcendentals=0)


def load(grad_out, momentum, pair, band):
    tokens, columns = grad_out.shape
    rows = momentum.shape[1]
    kept = columns // GROUP * band
    return pl.pallas_call(
        functools.partial(load_kernel, band),
        in_specs=[VMEM] * 3,
        out_specs=[VMEM] * 3,
        out_shape=[
            pltpu.VMEM((2 * kept, tokens), BF16),
            pltpu.VMEM((rows, columns), F32),
            pltpu.VMEM((kept, rows), F32),
        ],
        compiler_params=params(16),
        cost_estimate=estimate(2 * columns * (tokens + rows) * 256, 0),
        name="load",
    )(held(grad_out), held(momentum), pair)


def flat(chunks):
    pieces = [piece for chunk in chunks for piece in chunk]
    return tuple(map(len, chunks)), pieces, len(pieces), sum(piece.shape[0] for piece in pieces)


def add(places, xs, grad_in, coded, total, kept):
    groups, xs, count, tokens = flat(xs)
    rows, columns = total.shape
    return pl.pallas_call(
        functools.partial(add_kernel, groups),
        in_specs=[SMEM] + [VMEM] * (count + 4),
        out_specs=[VMEM] * 2,
        out_shape=[pltpu.VMEM(total.shape, F32), pltpu.VMEM(kept.shape, F32)],
        input_output_aliases={count + 3: 0, count + 4: 1},
        compiler_params=params(16),
        cost_estimate=estimate(2 * tokens * rows * columns * 5 // 4, 0),
        name="add",
    )(places, *[held(x) for x in xs], held(grad_in), held(coded), held(total), held(kept))


def code(places, core, xs, coded, kept):
    groups, xs, count, tokens = flat(xs)
    size, rows = kept.shape
    out = jax.ShapeDtypeStruct((size * rows // 256, 128), F32)
    return pl.pallas_call(
        functools.partial(code_kernel, groups),
        in_specs=[SMEM, SMEM] + [VMEM] * (count + 2),
        out_specs=[VMEM] * 3,
        out_shape=[pltpu.VMEM(kept.shape, F32), pltpu.VMEM(out.shape, F32), pltpu.VMEM(out.shape, F32)],
        compiler_params=params(16),
        cost_estimate=estimate(2 * tokens * rows * size * 2, 0),
        name="code",
    )(places, core, *[held(x) for x in xs], held(coded), held(kept))


def finish(places, xs, grad_in, total, kept, stacked, band):
    groups, xs, count, tokens = flat(xs)
    rows, columns = total.shape
    return pl.pallas_call(
        functools.partial(fresh_kernel, groups, band),
        in_specs=[SMEM] + [VMEM] * (count + 4),
        out_specs=ANY,
        out_shape=jax.ShapeDtypeStruct((1, rows, columns), BF16),
        scratch_shapes=[pltpu.VMEM((rows, columns), BF16), pltpu.SemaphoreType.DMA((rows // TILE,))],
        compiler_params=params(16),
        cost_estimate=estimate(4 * tokens * rows * columns, rows * columns * 2),
        name="finish",
    )(places, *[held(x) for x in xs], held(grad_in), held(total), held(kept), stacked)


def sum_parts(parts, chips):
    return pl.pallas_call(
        functools.partial(part_kernel, chips),
        in_specs=[VMEM],
        out_specs=VMEM,
        out_shape=jax.ShapeDtypeStruct(parts.shape, F32),
        compiler_params=params(16),
        name="sum_parts",
    )(parts)


def make_update(core, mine, other, stacked, band, rows, columns):
    return pl.pallas_call(
        functools.partial(update_kernel, band),
        grid=(2,),
        in_specs=[SMEM]
        + [pl.BlockSpec(mine.shape, lambda i: (0, 0))] * 2
        + [pl.BlockSpec(stacked.shape, lambda i: (0, 0))],
        out_specs=pl.BlockSpec((rows // 2, columns), lambda i: (i, 0)),
        out_shape=jax.ShapeDtypeStruct((rows, columns), BF16),
        compiler_params=params(32),
        name="update",
    )(core, mine, other, stacked)


def shards(x_rows, grad_out, momentum, band_index):
    band = band_index.shape[0]
    basis = dct_rows(band_index, GROUP)
    rounded = lax.reduce_precision(basis, 8, 7)
    high, low = rounded.astype(BF16), (basis - rounded).astype(BF16)
    pair = jnp.concatenate([high, low], axis=0)
    stacked = jnp.concatenate([high, high, low], axis=0)

    y, xl = lax.axis_index("y"), lax.axis_index("xl")
    core = lax.axis_index("core").astype(jnp.int32).reshape(1)

    def places(*steps):
        return jnp.stack([((y + dy) % 4) * 2 + (xl + dx) % 2 for dy, dx in steps]).astype(jnp.int32)

    def across(v):
        return lax.ppermute(v, "xl", PAIR)

    def from_above(v):
        return lax.ppermute(v, "y", ring(4, -1))

    def from_below(v):
        return lax.ppermute(v, "y", ring(4, 1))

    near = places((0, 0), (0, 1), (1, 0), (3, 0))
    middle = places((1, 1), (3, 1), (2, 0))
    last = places((2, 1))
    pair, stacked, near, middle, last, core = lax.optimization_barrier((pair, stacked, near, middle, last, core))
    with jax.named_scope("gather_near"):
        xn, yp, ym = across(x_rows), from_above(x_rows), from_below(x_rows)
        sums = load(grad_out, momentum, pair, band)
        (xn, yp, ym), (coded, total, kept) = lax.optimization_barrier(((xn, yp, ym), sums))
    with jax.named_scope("gather_middle"):
        xyp, xym, y2 = lax.optimization_barrier((across(yp), from_below(xn), from_above(yp)))
    total, kept = add(near, [[x_rows], [xn], [yp], [ym]], grad_out, coded, total, kept)
    with jax.named_scope("gather_far"):
        cuts = (96, 176)
        xy2 = [across(y2[: cuts[0]]), from_above(xyp[cuts[0] : cuts[1]]), from_below(xym[cuts[1] :])]
    total, kept = add(middle, [[xyp], [xym], [y2]], grad_out, coded, total, kept)
    kept, mine, other = code(last, core, [xy2], coded, kept)
    with jax.named_scope("sum_core"):
        mine = mine + lax.ppermute(other, "core", PAIR)
    fresh = finish(last, [xy2], grad_out, total, kept, stacked, band)
    with jax.named_scope("sum_chips"):
        parts = lax.all_to_all(mine, ("z", "xh"), 0, 0, tiled=True)
    with jax.named_scope("spread_chips"):
        whole = lax.all_to_all(sum_parts(parts, 16), ("z", "xh"), 0, 0, tiled=True)
    with jax.named_scope("spread_core"):
        other = lax.ppermute(whole, "core", PAIR)
    return fresh, make_update(core, whole, other, stacked, band, *total.shape)


def solution(mesh):
    fine = Mesh(mesh.devices.reshape(8, 2, 2, 4, 2), ("z", "xh", "core", "y", "xl"))
    rep, col = ("z", "xh", "core"), ("y", "xl")
    return jax.shard_map(
        shards,
        mesh=fine,
        in_specs=(P(rep + col, None), P(rep, col), P(rep, None, col), P()),
        out_specs=(P(rep, None, col), P(None, col)),
        check_vma=False,
    )
```

time: 431 us -> 97.9 us (0.23)
  waiting for transfers between devices: 358 us -> 11.8 us
  blocking collectives: 0 us -> 44.2 us
  matrix products: 33.4 us -> 0 us
  Pallas kernels: 0 us -> 18.2 us
  starting transfers between devices: 0.04 us -> 16.3 us
  between operations: 14.1 us -> 0.73 us
  local copies, waits for them, and re-layouts: 16 us -> 4.72 us
  other arithmetic: 8.67 us -> 1.72 us
    psum x1 -> x0, waiting for transfers between devices: 259 us -> none  [shards(): summed = lax.psum(coefficients, 'rep')]
    all_gather x1 -> x0, waiting for transfers between devices: 97.4 us -> none  [shards(): lax.all_gather(x_rows, 'col', axis=0, tiled=True)]
    all_to_all x0 -> x2, blocking collectives: none -> 44.2 us  [the longest x1 25.2 us: shards(): parts = lax.all_to_all(mine, ('z', 'xh'), 0, 0, tiled=True)]
    dot_general x4 -> x0, matrix products: 33.4 us -> none  [the longest x2 14.8 us: decode(): jnp.einsum('ibk,kn->ibn', coefficients, basis, precision=lax.Precision.HI...]
    pallas_call x0 -> x7, Pallas kernels: none -> 18.2 us  [the longest x2 9.36 us: add(): pl.pallas_call(functools.partial(add_kernel, groups), in_specs=[SMEM] + [...]
    ppermute x0 -> x11, starting transfers between devices: none -> 16.3 us  [the longest x3 7.89 us: from_above(): return lax.ppermute(v, 'y', ring(4, -1))]
    ppermute x0 -> x11, waiting for transfers between devices: none -> 11.8 us  [the longest x3 7.4 us: from_below(): return lax.ppermute(v, 'y', ring(4, 1))]
    broadcast_in_dim x1 -> x0, other arithmetic: 7.35 us -> none  [shards(): fresh[None]]
  transfers between devices with their start and end apart: 2 -> 11, of which waited for: 2 -> 7; matrix products, arithmetic and copies ran while one was open for 4% -> 2% of each run, Pallas kernels for 0% -> 16%
where the time goes in v1:
time: 97.9 us; the launch traced here: 97.7 us
  blocking collectives  44.2 us (45%)
  Pallas kernels  18.2 us (19%)
  starting transfers between devices  16.3 us (17%)
  waiting for transfers between devices  11.8 us (12%)
  local copies, waits for them, and re-layouts  4.72 us (5%)
  other arithmetic  1.72 us (2%)
    all_to_all x1, blocking collectives, shards(): parts = lax.all_to_all(mine, ('z', 'xh'), 0, 0, tiled=True)  25.2 us
    all_to_all x1, blocking collectives, shards(): whole = lax.all_to_all(sum_parts(parts, 16), ('z', 'xh'), 0, 0, tiled=True)  18.9 us
    pallas_call x2, Pallas kernels, add(): pl.pallas_call(functools.partial(add_kernel, groups), in_specs=[SMEM] + [...  9.36 us
    ppermute x3, starting transfers between devices, from_above(): return lax.ppermute(v, 'y', ring(4, -1))  7.89 us
    ppermute x3, waiting for transfers between devices, from_below(): return lax.ppermute(v, 'y', ring(4, 1))  7.4 us
    ppermute x1, starting transfers between devices, shards(): mine = mine + lax.ppermute(other, 'core', PAIR)  4.88 us
    unnamed x10, local copies, waits for them, and re-layouts  4.68 us
    pallas_call x1, Pallas kernels, finish(): pl.pallas_call(functools.partial(fresh_kernel, groups, band), in_specs=[S...  3.07 us
  transfers between devices with their start and end apart: 11, of which 7 were waited for; matrix products, arithmetic and copies ran while one was open for 2% of the time, Pallas kernels for 16%

profile of v1, /device:TPU:1, one launch (start us, length us, event | category | flops | bytes accessed | tf_op | source)
XLA Modules:
  0.0 97.7 jit_solution(12200834314855778668)
XLA Ops:
  0.6 3.6 %collective-permute-start.1 = (bf16[256,1024]{1,0:T(8,128)(2,1)}, bf16[256,1024]{1,0:T(8,128)(2,1)S(1)}, u32[]{:S(2)}, u32[]{:S(2)}) collective-permute-start(bf16[256,1024]{1,0:T(8,128)(2,1)} %refs_0_.1), channel_id=1, source_target_pairs={{0,6},{2,0},{4,2},{6,4},{1,7},{3,1},{5,3},{7,5},{8,14},{10,8},{12,... | collective-permute-start | bytes 1572872 | tf_op jit(solution)/shard_map/gather_near/ppermute | solution.py:293
  4.3 1.2 %collective-permute-start = (bf16[256,1024]{1,0:T(8,128)(2,1)}, bf16[256,1024]{1,0:T(8,128)(2,1)S(1)}, u32[]{:S(2)}, u32[]{:S(2)}) collective-permute-start(bf16[256,1024]{1,0:T(8,128)(2,1)} %refs_0_.1), channel_id=1, source_target_pairs={{0,1},{1,0},{2,3},{3,2},{4,5},{5,4},{6,7},{7,6},{8,9},{9,8},{10,11... | collective-permute-start | bytes 1572872 | tf_op jit(solution)/shard_map/gather_near/ppermute | solution.py:290
  5.5 0.7 convert_element_type.9
  6.1 0.7 compare_select_fusion
  7.2 2.8 %copy-done = bf16[2048,1536]{1,0:T(8,128)(2,1)S(1)} copy-done((bf16[2048,1536]{1,0:T(8,128)(2,1)S(1)}, bf16[2048,1536]{1,0:T(8,128)(2,1)}, u32[]{:S(2)}) %copy-start) | copy-done | bytes 6291480
  10.0 1.9 %copy-done.1 = bf16[1,1024,1536]{2,1,0:T(8,128)(2,1)S(1)} copy-done((bf16[1,1024,1536]{2,1,0:T(8,128)(2,1)S(1)}, bf16[1,1024,1536]{2,1,0:T(8,128)(2,1)}, u32[]{:S(2)}) %copy-start.1) | copy-done | bytes 3145752
  11.9 3.0 %load.1 = (bf16[384,2048]{1,0:T(8,128)(2,1)S(1)}, f32[1024,1536]{1,0:T(8,128)S(1)}, f32[192,1024]{1,0:T(8,128)S(1)}) custom-call(bf16[2048,1536]{1,0:T(8,128)(2,1)S(1)} %copy-done, bf16[1,1024,1536]{2,1,0:T(8,128)(2,1)S(1)} %copy-done.1, bf16[64,256]{1,0:T(8,128)(2,1)S(1)} %pad_maximum_fusion.1.pair), custom_call_target="tpu_custom_call" | custom-call | flops 2415919104 | tf_op jit(solution)/shard_map/gather_near/load/pallas_call | solution.py:185
  15.2 1.8 %collective-permute-done.refs_1_ = bf16[256,1024]{1,0:T(8,128)(2,1)S(1)} collective-permute-done((bf16[256,1024]{1,0:T(8,128)(2,1)}, bf16[256,1024]{1,0:T(8,128)(2,1)S(1)}, u32[]{:S(2)}, u32[]{:S(2)}) %collective-permute-start) | collective-permute-done | bytes 524320 | tf_op jit(solution)/shard_map/gather_near/ppermute | solution.py:290
  17.0 2.1 %collective-permute-done.2.refs_3_ = bf16[256,1024]{1,0:T(8,128)(2,1)S(1)} collective-permute-done((bf16[256,1024]{1,0:T(8,128)(2,1)}, bf16[256,1024]{1,0:T(8,128)(2,1)S(1)}, u32[]{:S(2)}, u32[]{:S(2)}) %collective-permute-start.2) | collective-permute-done | bytes 524320 | tf_op jit(solution)/shard_map/gather_near/ppermute | solution.py:296
  19.1 2.7 %collective-permute-start.5 = (bf16[256,1024]{1,0:T(8,128)(2,1)S(1)}, bf16[256,1024]{1,0:T(8,128)(2,1)S(1)}, u32[]{:S(2)}, u32[]{:S(2)}) collective-permute-start(bf16[256,1024]{1,0:T(8,128)(2,1)S(1)} %collective-permute-done.1.refs_2_), channel_id=1, source_target_pairs={{0,6},{2,0},{4,2},{6,4},{1,7},{3,1},{5,3},{7,5},{8,14},{10,8},{12,... | collective-permute-start | bytes 1572872 | tf_op jit(solution)/shard_map/gather_middle/ppermute | solution.py:293
  22.0 5.2 %add.120 = (f32[1024,1536]{1,0:T(8,128)S(1)}, f32[192,1024]{1,0:T(8,128)S(1)}) custom-call(s32[4]{0:T(128)S(1)} %pad_add_fusion.places, bf16[256,1024]{1,0:T(8,128)(2,1)S(1)} %copy-done.2, bf16[256,1024]{1,0:T(8,128)(2,1)S(1)} %collective-permute-done.refs_1_, ...), custom_call_target="tpu_custom_call", output_to_operand_aliasing={{0}: (7, {}), {1}: (8, {})} | custom-call | flops 4026531840 | tf_op jit(solution)/shard_map/add/pallas_call | solution.py:208
  27.2 4.3 %collective-permute-done.4.refs_1_ = bf16[256,1024]{1,0:T(8,128)(2,1)S(1)} collective-permute-done((bf16[256,1024]{1,0:T(8,128)(2,1)S(1)}, bf16[256,1024]{1,0:T(8,128)(2,1)S(1)}, u32[]{:S(2)}, u32[]{:S(2)}) %collective-permute-start.4) | collective-permute-done | bytes 524320 | tf_op jit(solution)/shard_map/gather_middle/ppermute | solution.py:296
  31.6 0.9 collective-permute-done.3.refs_0_
  32.5 1.6 %collective-permute-start.7 = (bf16[80,1024]{1,0:T(8,128)(2,1)S(1)}, bf16[80,1024]{1,0:T(8,128)(2,1)S(1)}, u32[]{:S(2)}, u32[]{:S(2)}) collective-permute-start(bf16[80,1024]{1,0:T(8,128)(2,1)S(1)} %slice.10), channel_id=1, source_target_pairs={{0,6},{2,0},{4,2},{6,4},{1,7},{3,1},{5,3},{7,5},{8,14},{10,8},{12,... | collective-permute-start | bytes 491528 | tf_op jit(solution)/shard_map/gather_far/ppermute | solution.py:293
  34.3 4.2 %add.121 = (f32[1024,1536]{1,0:T(8,128)S(1)}, f32[192,1024]{1,0:T(8,128)S(1)}) custom-call(s32[3]{0:T(128)S(1)} %pad_add_fusion.1.places, bf16[256,1024]{1,0:T(8,128)(2,1)S(1)} %collective-permute-done.3.refs_0_, bf16[256,1024]{1,0:T(8,128)(2,1)S(1)} %collective-permute-done.4.refs_1_, ...), custom_call_target="tpu_custom_call", output_to_operand_aliasing={{0}: (6, {}), {1}: (7, {})} | custom-call | flops 3019898880 | tf_op jit(solution)/shard_map/add/pallas_call | solution.py:208
  38.5 1.0 collective-permute-done.8.refs_2_
  39.5 0.4 code.1
  39.9 4.9 %collective-permute-start.9 = (f32[768,128]{1,0:T(8,128)S(1)}, f32[768,128]{1,0:T(8,128)S(1)}, u32[]{:S(2)}, u32[]{:S(2)}) collective-permute-start(f32[768,128]{1,0:T(8,128)S(1)} %get-tuple-element.51), channel_id=1, source_target_pairs={{0,8},{8,0},{1,9},{9,1},{2,10},{10,2},{3,11},{11,3},{4,12},{12,4},... | collective-permute-start | bytes 1179656 | tf_op jit(solution)/shard_map/sum_core/ppermute | solution.py:315
  44.7 1.3 %collective-permute-done.9 = f32[768,128]{1,0:T(8,128)S(1)} collective-permute-done((f32[768,128]{1,0:T(8,128)S(1)}, f32[768,128]{1,0:T(8,128)S(1)}, u32[]{:S(2)}, u32[]{:S(2)}) %collective-permute-start.9) | collective-permute-done | bytes 393248 | tf_op jit(solution)/shard_map/sum_core/ppermute | solution.py:315
  46.1 25.2 %all_to_all.22 = f32[16,48,128]{2,1,0:T(8,128)S(1)} all-to-all(f32[16,48,128]{2,1,0:T(8,128)S(1)} %bitcast.19), channel_id=1, replica_groups=mesh['z'=8,'xh'=2,'core'=2,'y'=4,'xl'=2] {'z','xh'}, dimensions={0} | all-to-all | bytes 786432 | tf_op jit(solution)/shard_map/sum_chips/all_to_all | solution.py:318
  71.4 18.9 %all_to_all.23 = f32[16,48,128]{2,1,0:T(8,128)S(1)} all-to-all(f32[16,48,128]{2,1,0:T(8,128)S(1)} %bitcast.18), channel_id=1, replica_groups=mesh['z'=8,'xh'=2,'core'=2,'y'=4,'xl'=2] {'z','xh'}, dimensions={0} | all-to-all | bytes 786432 | tf_op jit(solution)/shard_map/spread_chips/all_to_all | solution.py:320
  90.4 1.9 %collective-permute-start.10 = (f32[768,128]{1,0:T(8,128)S(1)}, f32[768,128]{1,0:T(8,128)S(1)}, u32[]{:S(2)}, u32[]{:S(2)}) collective-permute-start(f32[768,128]{1,0:T(8,128)S(1)} %bitcast.15), channel_id=1, source_target_pairs={{0,8},{8,0},{1,9},{9,1},{2,10},{10,2},{3,11},{11,3},{4,12},{12,4},... | collective-permute-start | bytes 1179656 | tf_op jit(solution)/shard_map/spread_core/ppermute | solution.py:322
  92.2 3.1 %finish.1 = bf16[1,1024,1536]{2,1,0:T(8,128)(2,1)} custom-call(s32[1]{0:T(128)} %bitcast.7.places, bf16[96,1024]{1,0:T(8,128)(2,1)S(1)} %collective-permute-done.6.refs_0_, bf16[80,1024]{1,0:T(8,128)(2,1)S(1)} %collective-permute-done.7.refs_1_, bf16[80,1024]{1,0:T(8,128)(2,1)S(1)} %collective-permute-done.8.refs_2_, bf16[2048,1536]{1,0:T(8,128)(2,1)S(1)} %bitcast.14, ...), custom_call_target="tpu_custom_call" | custom-call | flops 1610612736 | bytes 3145728 | tf_op jit(solution)/shard_map/finish/pallas_call | solution.py:238
  95.3 2.4 %update.1 = bf16[1024,1536]{1,0:T(8,128)(2,1)} custom-call(s32[1]{0:T(128)} %bitcast.8.core, f32[768,128]{1,0:T(8,128)S(1)} %bitcast.16, f32[768,128]{1,0:T(8,128)S(1)} %collective-permute-done.10.other, bf16[96,256]{1,0:T(8,128)(2,1)S(1)} %pad_maximum_fusion.refs_6_.stacked), custom_call_target="tpu_custom_call" | custom-call | tf_op jit(solution)/shard_map/update/pallas_call | solution.py:262
  (30 shorter events, 1.4 us)
Async XLA Ops:
  0.6 14.5 %collective-permute-start.1 = (bf16[256,1024]{1,0:T(8,128)(2,1)}, bf16[256,1024]{1,0:T(8,128)(2,1)S(1)}, u32[]{:S(2)}, u32[]{:S(2)}) collective-permute-start(bf16[256,1024]{1,0:T(8,128)(2,1)} %refs_0_.1), channel_id=1, source_target_pairs={{0,6},{2,0},{4,2},{6,4},{1,7},{3,1},{5,3},{7,5},{8,14},{10,8},{12,... | collective-permute-start | bytes 1572872 | tf_op jit(solution)/shard_map/gather_near/ppermute | solution.py:293
  4.3 12.7 %collective-permute-start = (bf16[256,1024]{1,0:T(8,128)(2,1)}, bf16[256,1024]{1,0:T(8,128)(2,1)S(1)}, u32[]{:S(2)}, u32[]{:S(2)}) collective-permute-start(bf16[256,1024]{1,0:T(8,128)(2,1)} %refs_0_.1), channel_id=1, source_target_pairs={{0,1},{1,0},{2,3},{3,2},{4,5},{5,4},{6,7},{7,6},{8,9},{9,8},{10,11... | collective-permute-start | bytes 1572872 | tf_op jit(solution)/shard_map/gather_near/ppermute | solution.py:290
  5.5 13.6 %collective-permute-start.2 = (bf16[256,1024]{1,0:T(8,128)(2,1)}, bf16[256,1024]{1,0:T(8,128)(2,1)S(1)}, u32[]{:S(2)}, u32[]{:S(2)}) collective-permute-start(bf16[256,1024]{1,0:T(8,128)(2,1)} %refs_0_.1), channel_id=1, source_target_pairs={{0,2},{2,4},{4,6},{6,0},{1,3},{3,5},{5,7},{7,1},{8,10},{10,12},{12... | collective-permute-start | bytes 1572872 | tf_op jit(solution)/shard_map/gather_near/ppermute | solution.py:296
  7.2 2.8 %copy-start = (bf16[2048,1536]{1,0:T(8,128)(2,1)S(1)}, bf16[2048,1536]{1,0:T(8,128)(2,1)}, u32[]{:S(2)}) copy-start(bf16[2048,1536]{1,0:T(8,128)(2,1)} %refs_3_.3) | copy-start | bytes 18874372
  10.0 1.9 %copy-start.1 = (bf16[1,1024,1536]{2,1,0:T(8,128)(2,1)S(1)}, bf16[1,1024,1536]{2,1,0:T(8,128)(2,1)}, u32[]{:S(2)}) copy-start(bf16[1,1024,1536]{2,1,0:T(8,128)(2,1)} %momentum.1) | copy-start | bytes 9437188
  11.9 10.2 %copy-start.2 = (bf16[256,1024]{1,0:T(8,128)(2,1)S(1)}, bf16[256,1024]{1,0:T(8,128)(2,1)}, u32[]{:S(2)}) copy-start(bf16[256,1024]{1,0:T(8,128)(2,1)} %refs_0_.1) | copy-start | bytes 1572868
  19.1 12.5 %collective-permute-start.4 = (bf16[256,1024]{1,0:T(8,128)(2,1)S(1)}, bf16[256,1024]{1,0:T(8,128)(2,1)S(1)}, u32[]{:S(2)}, u32[]{:S(2)}) collective-permute-start(bf16[256,1024]{1,0:T(8,128)(2,1)S(1)} %collective-permute-done.refs_1_), channel_id=1, source_target_pairs={{0,2},{2,4},{4,6},{6,0},{1,3},{3,5},{5,7},{7,1},{8,10},{10,12},{12... | collective-permute-start | bytes 1572872 | tf_op jit(solution)/shard_map/gather_middle/ppermute | solution.py:296
  19.1 12.5 %collective-permute-start.5 = (bf16[256,1024]{1,0:T(8,128)(2,1)S(1)}, bf16[256,1024]{1,0:T(8,128)(2,1)S(1)}, u32[]{:S(2)}, u32[]{:S(2)}) collective-permute-start(bf16[256,1024]{1,0:T(8,128)(2,1)S(1)} %collective-permute-done.1.refs_2_), channel_id=1, source_target_pairs={{0,6},{2,0},{4,2},{6,4},{1,7},{3,1},{5,3},{7,5},{8,14},{10,8},{12,... | collective-permute-start | bytes 1572872 | tf_op jit(solution)/shard_map/gather_middle/ppermute | solution.py:293
  21.8 10.7 %collective-permute-start.3 = (bf16[256,1024]{1,0:T(8,128)(2,1)S(1)}, bf16[256,1024]{1,0:T(8,128)(2,1)S(1)}, u32[]{:S(2)}, u32[]{:S(2)}) collective-permute-start(bf16[256,1024]{1,0:T(8,128)(2,1)S(1)} %collective-permute-done.1.refs_2_), channel_id=1, source_target_pairs={{0,1},{1,0},{2,3},{3,2},{4,5},{5,4},{6,7},{7,6},{8,9},{9,8},{10,11... | collective-permute-start | bytes 1572872 | tf_op jit(solution)/shard_map/gather_middle/ppermute | solution.py:290
  32.5 6.0 %collective-permute-start.7 = (bf16[80,1024]{1,0:T(8,128)(2,1)S(1)}, bf16[80,1024]{1,0:T(8,128)(2,1)S(1)}, u32[]{:S(2)}, u32[]{:S(2)}) collective-permute-start(bf16[80,1024]{1,0:T(8,128)(2,1)S(1)} %slice.10), channel_id=1, source_target_pairs={{0,6},{2,0},{4,2},{6,4},{1,7},{3,1},{5,3},{7,5},{8,14},{10,8},{12,... | collective-permute-start | bytes 491528 | tf_op jit(solution)/shard_map/gather_far/ppermute | solution.py:293
  34.1 5.4 %collective-permute-start.8 = (bf16[80,1024]{1,0:T(8,128)(2,1)S(1)}, bf16[80,1024]{1,0:T(8,128)(2,1)S(1)}, u32[]{:S(2)}, u32[]{:S(2)}) collective-permute-start(bf16[80,1024]{1,0:T(8,128)(2,1)S(1)} %slice.11), channel_id=1, source_target_pairs={{0,2},{2,4},{4,6},{6,0},{1,3},{3,5},{5,7},{7,1},{8,10},{10,12},{12... | collective-permute-start | bytes 491528 | tf_op jit(solution)/shard_map/gather_far/ppermute | solution.py:296
  34.1 5.4 %collective-permute-start.6 = (bf16[96,1024]{1,0:T(8,128)(2,1)S(1)}, bf16[96,1024]{1,0:T(8,128)(2,1)S(1)}, u32[]{:S(2)}, u32[]{:S(2)}) collective-permute-start(bf16[96,1024]{1,0:T(8,128)(2,1)S(1)} %slice.9), channel_id=1, source_target_pairs={{0,1},{1,0},{2,3},{3,2},{4,5},{5,4},{6,7},{7,6},{8,9},{9,8},{10,11... | collective-permute-start | bytes 589832 | tf_op jit(solution)/shard_map/gather_far/ppermute | solution.py:290
  34.3 57.9 %slice-start = ((s8[6291456]{0:T(1024)(128)(4,1)}), s8[4194304]{0:T(1024)(128)(4,1)S(1)}, s32[]{:S(2)}) async-start(s8[6291456]{0:T(1024)(128)(4,1)} %bitcast.13), calls=%async_computation.2 | async-start | bytes 8388608
  34.3 57.9 %slice-start.1 = ((s8[6291456]{0:T(1024)(128)(4,1)}), s8[2097152]{0:T(1024)(128)(4,1)S(1)}, s32[]{:S(2)}) async-start(s8[6291456]{0:T(1024)(128)(4,1)} %bitcast.13), calls=%async_computation.3 | async-start | bytes 4194304
  39.9 6.2 %collective-permute-start.9 = (f32[768,128]{1,0:T(8,128)S(1)}, f32[768,128]{1,0:T(8,128)S(1)}, u32[]{:S(2)}, u32[]{:S(2)}) collective-permute-start(f32[768,128]{1,0:T(8,128)S(1)} %get-tuple-element.51), channel_id=1, source_target_pairs={{0,8},{8,0},{1,9},{9,1},{2,10},{10,2},{3,11},{11,3},{4,12},{12,4},... | collective-permute-start | bytes 1179656 | tf_op jit(solution)/shard_map/sum_core/ppermute | solution.py:315
  90.4 4.9 %collective-permute-start.10 = (f32[768,128]{1,0:T(8,128)S(1)}, f32[768,128]{1,0:T(8,128)S(1)}, u32[]{:S(2)}, u32[]{:S(2)}) collective-permute-start(f32[768,128]{1,0:T(8,128)S(1)} %bitcast.15), channel_id=1, source_target_pairs={{0,8},{8,0},{1,9},{9,1},{2,10},{10,2},{3,11},{11,3},{4,12},{12,4},... | collective-permute-start | bytes 1179656 | tf_op jit(solution)/shard_map/spread_core/ppermute | solution.py:322

commit v2 on v1

v2 whole, which is shorter than its diff:
```python
import functools
import math

import jax
import jax.numpy as jnp
from jax import lax
from jax.experimental import pallas as pl
from jax.experimental.pallas import tpu as pltpu
from jax.sharding import Mesh
from jax.sharding import PartitionSpec as P

GROUP = 256
TILE = 512
PAD = 16
F32 = jnp.float32
BF16 = jnp.bfloat16
PAIR = [(0, 1), (1, 0)]


def ring(size, step):
    return [(i, (i + step) % size) for i in range(size)]


def dct_rows(band, length):
    index = band.astype(F32)[:, None]
    cells = jnp.arange(length, dtype=F32)[None, :]
    factor = jnp.where(band == 0, math.sqrt(1.0 / length), math.sqrt(2.0 / length)).astype(F32)
    return factor[:, None] * jnp.cos(math.pi * (cells + 0.5) * index / length)


def split(value):
    high = value.astype(BF16)
    return high, (value - high.astype(F32)).astype(BF16)


def dot(a, b, dims):
    return lax.dot_general(a, b, ((dims[:1], dims[1:]), ((), ())), preferred_element_type=F32)


def decode(coefficients, stacked):
    high, low = split(coefficients)
    return dot(jnp.concatenate([high, low, high], axis=0), stacked, (0, 0))


def encode(pair, values, band):
    both = dot(pair, values, (1, 1))
    return both[:band] + both[band:]


def block(index, size):
    return slice(index * size, (index + 1) * size)


def load_kernel(band, place, grad_out, momentum, pair, x_rows, coded, kept, own, grad_in, total, momentum_in, sems):
    blocks = grad_in.shape[1] // GROUP
    halves = [block(h, grad_in.shape[0] // 2) for h in range(2)]
    ends = [(momentum.at[0], momentum_in)] + [(grad_out.at[h], grad_in.at[h]) for h in halves] + [(x_rows, own)]
    copies = [pltpu.make_async_copy(*pair, sems.at[c]) for c, pair in enumerate(ends)]
    for copy in copies:
        copy.start()
    copies[0].wait()
    for b in range(blocks):
        kept[block(b, band), :] = 0.9 * encode(pair[...], momentum_in[:, block(b, GROUP)], band)
    for copy, half in zip(copies[1:3], halves):
        copy.wait()
        for b in range(blocks):
            high, low = split(encode(pair[...], grad_in[half, block(b, GROUP)], band))
            coded[block(b, band), half] = high
            coded[block(blocks + b, band), half] = low
    copies[3].wait()
    for i in range(total.shape[0] // TILE):
        rows = block(i, TILE)
        kept[:, rows] = kept[:, rows] + code_sum(place, [[own]], coded, rows)
        for w in range(total.shape[1] // TILE):
            wide = block(w, TILE)
            start = 0.9 * momentum_in[rows, wide].astype(F32)
            total[rows, wide] = start + grad_sum(place, [[own]], grad_in, rows, wide)


def tokens_of(place, count):
    return pl.ds(pl.multiple_of(place * count, count), count)


def chunks(groups, refs):
    taken, out = 0, []
    for count in groups:
        out.append(refs[taken : taken + count])
        taken += count
    return out, refs[taken:]


def take(pieces, columns):
    parts = [piece[:, columns] for piece in pieces]
    return parts[0] if len(parts) == 1 else jnp.concatenate(parts, axis=0)


def code_sum(places, xs, coded, columns):
    value = 0.0
    half = coded.shape[0] // 2
    for s, pieces in enumerate(xs):
        x = take(pieces, columns)
        tokens = tokens_of(places[s], x.shape[0])
        value = value + (dot(coded[:half, tokens], x, (1, 0)) + dot(coded[half:, tokens], x, (1, 0)))
    return value


def grad_sum(places, xs, grad_in, rows, columns):
    value = 0.0
    for s, pieces in enumerate(xs):
        x = take(pieces, rows)
        value = value + dot(x, grad_in[tokens_of(places[s], x.shape[0]), columns], (0, 0))
    return value


def add_kernel(groups, span, places, *refs):
    xs, refs = chunks(groups, refs)
    grad_in, base = refs[:2]
    total, staged, sems = refs[-3:]
    copies = []
    for w in range(total.shape[1] // TILE):
        wide = block(w, TILE)
        staged[:, wide] = base[span, wide] + grad_sum(places, xs, grad_in, span, wide)
        copies.append(pltpu.make_async_copy(staged.at[:, wide], total.at[span, wide], sems.at[w]))
        copies[-1].start()
    for copy in copies:
        copy.wait()


def tally_kernel(groups, places, *refs):
    xs, refs = chunks(groups, refs)
    coded, kept, kept_out = refs
    half = kept.shape[1] // 2
    for i in range(2):
        rows = block(i, half)
        kept_out[:, rows] = kept[:, rows] + code_sum(places, xs, coded, rows)


def code_kernel(groups, places, core, *refs):
    xs, refs = chunks(groups, refs)
    coded, kept, kept_out, mine, other = refs
    rows = kept.shape[1] // 2

    def half(index, out):
        columns = pl.ds(pl.multiple_of(index * rows, rows), rows)
        value = kept[:, columns] + code_sum(places, xs, coded, columns)
        kept_out[:, columns] = value
        for t in range(rows // 128):
            out[block(t, value.shape[0]), :] = value[:, block(t, 128)]

    half(1 - core[0], other)
    half(core[0], mine)


def fresh_kernel(groups, band, places, *refs):
    count = sum(groups)
    xs, refs = refs[:count], refs[count:]
    grad_out, total, kept, stacked, fresh, x_in, g_in, total_in, kept_in, staged, sems, out_sems = refs
    rows, columns = total.shape
    steps, wides = rows // TILE, columns // TILE
    tokens = x_in.shape[0] // len(groups)
    ends = []
    ready = [[0] * wides for _ in range(steps)]
    for i in range(steps):
        span, start = block(i, TILE), 0
        for x in xs:
            ends.append((x.at[:, span], x_in.at[start : start + x.shape[0], span]))
            start += x.shape[0]
        for w in range(wides):
            wide = block(w, TILE)
            for s in range(len(groups) if i == 0 else 0):
                ends.append((grad_out.at[tokens_of(places[s], tokens), wide], g_in.at[block(s, tokens), wide]))
            ends.append((total.at[span, wide], total_in.at[span, wide]))
            if w == 0:
                ends.append((kept.at[:, span], kept_in.at[:, span]))
            ready[i][w] = len(ends)
    copies = [pltpu.make_async_copy(*pair, sems.at[i]) for i, pair in enumerate(ends)]
    for copy in copies:
        copy.start()
    waited, outs = 0, []
    for i in range(steps):
        span = block(i, TILE)
        for w in range(wides):
            for copy in copies[waited : ready[i][w]]:
                copy.wait()
            waited = ready[i][w]
            for b in range(w * TILE // GROUP, (w + 1) * TILE // GROUP):
                cols = block(b, GROUP)
                value = total_in[span, cols] + dot(x_in[:, span], g_in[:, cols], (0, 0))
                value = value - decode(kept_in[block(b, band), span], stacked[...])
                staged[span, cols] = value.astype(BF16)
        outs.append(pltpu.make_async_copy(staged.at[span], fresh.at[0, span], out_sems.at[i]))
        outs[-1].start()
    for out in outs:
        out.wait()


def join_kernel(mine, other, kept, out, kept_out, staged, sems):
    save = pltpu.make_async_copy(kept, kept_out, sems.at[0])
    staged[...] = mine[...] + other[...]
    give = pltpu.make_async_copy(staged, out, sems.at[1])
    give.start()
    save.start()
    give.wait()
    save.wait()


def part_kernel(chips, parts, spread):
    rows = parts.shape[0] // chips
    value = parts[:rows, :]
    for i in range(1, chips):
        value = value + parts[block(i, rows), :]
    largest = jnp.maximum(jnp.max(jnp.abs(value), axis=0, keepdims=True), 2.0**-100)
    power = jnp.ceil(jnp.log2(largest))
    level = jnp.round(value * jnp.exp2(15.0 - power))
    level = jnp.clip(level, -32767.0, 32767.0).astype(jnp.int32).astype(jnp.int16)
    power = jnp.broadcast_to(power, (PAD, value.shape[1])).astype(jnp.int32).astype(jnp.int16)
    for i in range(chips):
        start = i * (rows + PAD)
        spread[start : start + rows, :] = level
        spread[start + rows : start + rows + PAD, :] = power


def update_kernel(band, chips, where, whole, stacked, *refs):
    update = refs[-1]
    rows = whole.shape[0] // chips - PAD
    values = []
    for i in range(chips):
        start = i * (rows + PAD)
        level = whole[start : start + rows, :].astype(jnp.int32).astype(F32)
        power = whole[start + rows : start + rows + PAD, :].astype(jnp.int32).astype(F32)[:1]
        values.append(level * jnp.exp2(power - 15.0))
    value = jnp.concatenate(values, axis=0)
    tiles = update.shape[0] // 128
    kept = value.shape[0] // tiles
    for b in range(update.shape[1] // GROUP):
        parts = [value[t * kept + b * band : t * kept + (b + 1) * band] for t in range(tiles)]
        update[:, block(b, GROUP)] = decode(jnp.concatenate(parts, axis=1), stacked[...]).astype(BF16)


VMEM = pl.BlockSpec(memory_space=pltpu.VMEM)
SMEM = pl.BlockSpec(memory_space=pltpu.SMEM)
ANY = pl.BlockSpec(memory_space=pl.ANY)
HBM = pl.BlockSpec(memory_space=pltpu.HBM)


def params(mib):
    return pltpu.CompilerParams(vmem_limit_bytes=mib << 20)


def held(value):
    return pltpu.with_memory_space_constraint(value, pltpu.VMEM)


def far(value):
    return pltpu.with_memory_space_constraint(value, pltpu.HBM)


def estimate(flops, size):
    return pl.CostEstimate(flops=flops, bytes_accessed=size, transcendentals=0)


def load(place, grad_out, momentum, pair, x_rows, band):
    tokens, columns = grad_out.shape
    rows = momentum.shape[1]
    kept = columns // GROUP * band
    return pl.pallas_call(
        functools.partial(load_kernel, band),
        in_specs=[SMEM, ANY, ANY, VMEM, ANY],
        out_specs=[VMEM] * 5,
        out_shape=[
            pltpu.VMEM((2 * kept, tokens), BF16),
            pltpu.VMEM((kept, rows), F32),
            pltpu.VMEM(x_rows.shape, BF16),
            pltpu.VMEM(grad_out.shape, BF16),
            pltpu.VMEM((rows, columns), F32),
        ],
        scratch_shapes=[pltpu.VMEM((rows, columns), BF16), pltpu.SemaphoreType.DMA((4,))],
        compiler_params=params(16),
        cost_estimate=estimate(2 * columns * (tokens + rows) * 256, 2 * columns * (tokens + rows)),
        name="load",
    )(place, far(grad_out), far(momentum), pair, far(x_rows))


def flat(chunks):
    pieces = [piece for chunk in chunks for piece in chunk]
    return tuple(map(len, chunks)), pieces, len(pieces), sum(piece.shape[0] for piece in pieces)


def add(span, places, xs, grad_in, base, total=None):
    groups, xs, count, tokens = flat(xs)
    shape = base.shape
    rows = span.stop - span.start
    others = [] if total is None else [far(total)]
    return pl.pallas_call(
        functools.partial(add_kernel, groups, span),
        in_specs=[SMEM] + [VMEM] * (count + 2) + [ANY] * len(others),
        out_specs=ANY,
        out_shape=pltpu.HBM(shape, F32),
        input_output_aliases={count + 3: 0} if others else {},
        scratch_shapes=[pltpu.VMEM((rows, shape[1]), F32), pltpu.SemaphoreType.DMA((shape[1] // TILE,))],
        compiler_params=params(16),
        cost_estimate=estimate(2 * tokens * rows * shape[1], rows * shape[1] * 4),
        name="add",
    )(places, *[held(x) for x in xs], held(grad_in), held(base), *others)


def tally(places, xs, coded, kept):
    groups, xs, count, tokens = flat(xs)
    size, rows = kept.shape
    return pl.pallas_call(
        functools.partial(tally_kernel, groups),
        in_specs=[SMEM] + [VMEM] * (count + 2),
        out_specs=VMEM,
        out_shape=pltpu.VMEM(kept.shape, F32),
        compiler_params=params(16),
        cost_estimate=estimate(2 * tokens * rows * size * 2, 0),
        name="tally",
    )(places, *[held(x) for x in xs], held(coded), held(kept))


def code(places, core, xs, coded, kept):
    groups, xs, count, tokens = flat(xs)
    size, rows = kept.shape
    out = jax.ShapeDtypeStruct((size * rows // 256, 128), F32)
    return pl.pallas_call(
        functools.partial(code_kernel, groups),
        in_specs=[SMEM, SMEM] + [VMEM] * (count + 2),
        out_specs=[VMEM] * 3,
        out_shape=[pltpu.VMEM(kept.shape, F32), pltpu.VMEM(out.shape, F32), pltpu.VMEM(out.shape, F32)],
        compiler_params=params(16),
        cost_estimate=estimate(2 * tokens * rows * size * 2, 0),
        name="code",
    )(places, core, *[held(x) for x in xs], held(coded), held(kept))


def finish(places, xs, grad_out, total, kept, stacked, band):
    groups, xs, count, tokens = flat(xs)
    rows, columns = total.shape
    steps, wides = rows // TILE, columns // TILE
    loads = (count + 1) * steps + wides * (len(groups) + steps)
    return pl.pallas_call(
        functools.partial(fresh_kernel, groups, band),
        in_specs=[SMEM] + [ANY] * (count + 3) + [VMEM],
        out_specs=ANY,
        out_shape=jax.ShapeDtypeStruct((1, rows, columns), BF16),
        scratch_shapes=[
            pltpu.VMEM((tokens, rows), BF16),
            pltpu.VMEM((tokens, columns), BF16),
            pltpu.VMEM(total.shape, F32),
            pltpu.VMEM(kept.shape, F32),
            pltpu.VMEM((rows, columns), BF16),
            pltpu.SemaphoreType.DMA((loads,)),
            pltpu.SemaphoreType.DMA((steps,)),
        ],
        compiler_params=params(24),
        cost_estimate=estimate(4 * tokens * rows * columns, rows * columns * 6),
        name="finish",
    )(places, *map(far, xs), far(grad_out), far(total), far(kept), stacked)


def join(mine, other, kept):
    return pl.pallas_call(
        join_kernel,
        in_specs=[VMEM] * 3,
        out_specs=[ANY] * 2,
        out_shape=[pltpu.HBM(mine.shape, F32), pltpu.HBM(kept.shape, F32)],
        scratch_shapes=[pltpu.VMEM(mine.shape, F32), pltpu.SemaphoreType.DMA((2,))],
        compiler_params=params(4),
        name="join",
    )(held(mine), held(other), held(kept))


def sum_parts(parts, chips):
    return pl.pallas_call(
        functools.partial(part_kernel, chips),
        in_specs=[VMEM],
        out_specs=VMEM,
        out_shape=pltpu.VMEM((parts.shape[0] + chips * PAD, parts.shape[1]), jnp.int16),
        compiler_params=params(16),
        name="sum_parts",
    )(held(parts))


def make_update(where, whole, stacked, band, rows, columns, update=None):
    others = [] if update is None else [update]
    return pl.pallas_call(
        functools.partial(update_kernel, band, 8),
        grid_spec=pltpu.PrefetchScalarGridSpec(
            num_scalar_prefetch=1,
            grid=(2,),
            in_specs=[
                pl.BlockSpec((whole.shape[0] // 2, whole.shape[1]), lambda i, where: (i, 0)),
                pl.BlockSpec(stacked.shape, lambda i, where: (0, 0)),
            ]
            + [ANY] * len(others),
            out_specs=pl.BlockSpec((rows // 4, columns), lambda i, where: (2 * where[0] + i, 0)),
        ),
        out_shape=jax.ShapeDtypeStruct((rows, columns), BF16),
        input_output_aliases={3: 0} if others else {},
        compiler_params=params(16),
        cost_estimate=estimate(rows * columns * 96, rows * columns),
        name="update",
    )(where, whole, stacked, *others)


def shards(x_rows, grad_out, momentum, band_index):
    band = band_index.shape[0]
    basis = dct_rows(band_index, GROUP)
    rounded = lax.reduce_precision(basis, 8, 7)
    high, low = rounded.astype(BF16), (basis - rounded).astype(BF16)
    pair = jnp.concatenate([high, low], axis=0)
    stacked = jnp.concatenate([high, high, low], axis=0)

    y, xl = lax.axis_index("y"), lax.axis_index("xl")
    core = lax.axis_index("core").astype(jnp.int32).reshape(1)

    def places(*steps):
        return jnp.stack([((y + dy) % 4) * 2 + (xl + dx) % 2 for dy, dx in steps]).astype(jnp.int32)

    def across(v):
        return lax.ppermute(v, "xl", PAIR)

    def from_above(v):
        return lax.ppermute(v, "y", ring(4, -1))

    def from_below(v):
        return lax.ppermute(v, "y", ring(4, 1))

    first = places((0, 0))
    near = places((0, 1), (1, 0), (3, 0))
    middle = places((1, 1), (3, 1), (2, 0))
    last = places((2, 1))
    ends = places((1, 1), (3, 1), (2, 0), (2, 1))
    apart = 1 - core
    pair, stacked, first, near, middle, last, ends, core, apart = lax.optimization_barrier(
        (pair, stacked, first, near, middle, last, ends, core, apart)
    )
    with jax.named_scope("gather_near"):
        yp, xn, ym = from_above(x_rows), across(x_rows), from_below(x_rows)
        loaded = load(first, grad_out, momentum, pair, x_rows, band)
        yp, (coded, kept, own, grad_in, base) = lax.optimization_barrier((yp, loaded))
        xn, ym = lax.optimization_barrier((xn, ym))
    half = yp.shape[0] // 2
    with jax.named_scope("gather_middle"):
        y2 = [from_above(yp[:half])]
        xyp = across(yp)
        y2.append(from_above(yp[half:]))
        xym = [from_below(xn[half:])]
        xym.insert(0, from_below(xn[:half]))
    rows = momentum.shape[1]
    close = [[xn], [yp], [ym]]
    total = add(slice(0, rows // 2), near, close, grad_in, base)
    y2[0], xym[1], total = lax.optimization_barrier((y2[0], xym[1], total))
    with jax.named_scope("gather_far"):
        xy2 = [across(y2[0]), from_below(xym[1])]
    total = add(slice(rows // 2, rows), near, close, grad_in, base, total)
    kept = tally(near, close, coded, kept)
    kept = tally(middle, [[xyp], xym, y2], coded, kept)
    kept, total = lax.optimization_barrier((kept, total))
    kept, mine, other = code(last, core, [xy2], coded, kept)
    with jax.named_scope("sum_core"):
        mine, kept = join(mine, lax.ppermute(other, "core", PAIR), kept)
    with jax.named_scope("sum_chips"):
        parts = lax.all_to_all(mine, ("z", "xh"), 0, 0, tiled=True)
    fresh = finish(ends, [[xyp], xym, y2, xy2], grad_out, total, kept, stacked, band)
    parts, fresh = lax.optimization_barrier((parts, fresh))
    with jax.named_scope("spread_chips"):
        whole = lax.all_to_all(sum_parts(parts, 16), ("z", "xh"), 0, 0, tiled=True)
    with jax.named_scope("spread_core"):
        other = lax.ppermute(whole, "core", PAIR)
    update = make_update(core, whole, stacked, band, rows, grad_out.shape[1])
    return fresh, make_update(apart, other, stacked, band, rows, grad_out.shape[1], update)


def solution(mesh):
    fine = Mesh(mesh.devices.reshape(8, 2, 2, 4, 2), ("z", "xh", "core", "y", "xl"))
    rep, col = ("z", "xh", "core"), ("y", "xl")
    return jax.shard_map(
        shards,
        mesh=fine,
        in_specs=(P(rep + col, None), P(rep, col), P(rep, None, col), P()),
        out_specs=(P(rep, None, col), P(None, col)),
        check_vma=False,
    )
```

time: 97.9 us -> 91.6 us (0.936)
  blocking collectives: 44.2 us -> 16.2 us
  Pallas kernels: 18.2 us -> 29.4 us
  starting transfers between devices: 16.3 us -> 25.6 us
  waiting for transfers between devices: 11.8 us -> 17.5 us
  local copies, waits for them, and re-layouts: 4.72 us -> 0.1 us
    all_to_all x1 -> x0, blocking collectives: 25.2 us -> none  [shards(): parts = lax.all_to_all(mine, ('z', 'xh'), 0, 0, tiled=True)]
    all_to_all x0 -> x1, starting transfers between devices: none -> 10.5 us  [shards(): parts = lax.all_to_all(mine, ('z', 'xh'), 0, 0, tiled=True)]
    pallas_call x1, Pallas kernels: 3.07 us -> 9.34 us  [finish(): pl.pallas_call(functools.partial(fresh_kernel, groups, band), in_specs=[S...]
    all_to_all x0 -> x1, waiting for transfers between devices: none -> 5.6 us  [shards(): parts = lax.all_to_all(mine, ('z', 'xh'), 0, 0, tiled=True)]
    pallas_call x4 -> x8, Pallas kernels: 14.7 us -> 19.6 us  [the longest x1 6.35 us: load(): pl.pallas_call(functools.partial(load_kernel, band), in_specs=[SMEM, ANY,...]
    unnamed x10 -> x14, local copies, waits for them, and re-layouts: 4.68 us -> 0.03 us
    all_to_all x1, blocking collectives: 18.9 us -> 16.2 us  [shards(): whole = lax.all_to_all(sum_parts(parts, 16), ('z', 'xh'), 0, 0, tiled=True)]
    ppermute x3, waiting for transfers between devices: 2.68 us -> 0.53 us  [across(): return lax.ppermute(v, 'xl', PAIR)]
  transfers between devices with their start and end apart: 11 -> 13, of which waited for: 7 -> 8; matrix products, arithmetic and copies ran while one was open for 2% -> 2% of each run, Pallas kernels for 16% -> 29%
where the time goes in v2:
time: 91.6 us; the launch traced here: 91.4 us
  Pallas kernels  29.4 us (32%)
  starting transfers between devices  25.6 us (28%)
  waiting for transfers between devices  17.5 us (19%)
  blocking collectives  16.2 us (18%)
  other arithmetic  1.68 us (2%)
    all_to_all x1, blocking collectives, shards(): whole = lax.all_to_all(sum_parts(parts, 16), ('z', 'xh'), 0, 0, tiled=True)  16.2 us
    all_to_all x1, starting transfers between devices, shards(): parts = lax.all_to_all(mine, ('z', 'xh'), 0, 0, tiled=True)  10.5 us
    pallas_call x1, Pallas kernels, finish(): pl.pallas_call(functools.partial(fresh_kernel, groups, band), in_specs=[S...  9.34 us
    ppermute x4, waiting for transfers between devices, from_below(): return lax.ppermute(v, 'y', ring(4, 1))  8.4 us
    ppermute x3, starting transfers between devices, from_above(): return lax.ppermute(v, 'y', ring(4, -1))  6.35 us
    pallas_call x1, Pallas kernels, load(): pl.pallas_call(functools.partial(load_kernel, band), in_specs=[SMEM, ANY,...  6.35 us
    pallas_call x2, Pallas kernels, add(): pl.pallas_call(functools.partial(add_kernel, groups, span), in_specs=[SME...  6.13 us
    all_to_all x1, waiting for transfers between devices, shards(): parts = lax.all_to_all(mine, ('z', 'xh'), 0, 0, tiled=True)  5.6 us
  transfers between devices with their start and end apart: 13, of which 8 were waited for; matrix products, arithmetic and copies ran while one was open for 2% of the time, Pallas kernels for 29%

profile of v2, /device:TPU:1, one launch (start us, length us, event | category | flops | bytes accessed | tf_op | source)
XLA Modules:
  0.0 91.4 jit_solution(7374415725385007452)
XLA Ops:
  0.6 3.6 %collective-permute-start = (bf16[256,1024]{1,0:T(8,128)(2,1)}, bf16[256,1024]{1,0:T(8,128)(2,1)S(1)}, u32[]{:S(2)}, u32[]{:S(2)}) collective-permute-start(bf16[256,1024]{1,0:T(8,128)(2,1)} %x_rows.1), channel_id=1, source_target_pairs={{0,6},{2,0},{4,2},{6,4},{1,7},{3,1},{5,3},{7,5},{8,14},{10,8},{12,... | collective-permute-start | bytes 1572872 | tf_op jit(solution)/shard_map/gather_near/ppermute | solution.py:424
  4.3 1.2 %collective-permute-start.2 = (bf16[256,1024]{1,0:T(8,128)(2,1)}, bf16[256,1024]{1,0:T(8,128)(2,1)S(1)}, u32[]{:S(2)}, u32[]{:S(2)}) collective-permute-start(bf16[256,1024]{1,0:T(8,128)(2,1)} %x_rows.1), channel_id=1, source_target_pairs={{0,1},{1,0},{2,3},{3,2},{4,5},{5,4},{6,7},{7,6},{8,9},{9,8},{10,11... | collective-permute-start | bytes 1572872 | tf_op jit(solution)/shard_map/gather_near/ppermute | solution.py:421
  7.2 6.3 %load.1 = (bf16[384,2048]{1,0:T(8,128)(2,1)S(1)}, f32[192,1024]{1,0:T(8,128)S(1)}, bf16[256,1024]{1,0:T(8,128)(2,1)}, bf16[2048,1536]{1,0:T(8,128)(2,1)S(1)}, f32[1024,1536]{1,0:T(8,128)S(1)}) custom-call(s32[1]{0:T(128)} %bitcast.place, bf16[2048,1536]{1,0:T(8,128)(2,1)} %refs_7_.1, bf16[1,1024,1536]{2,1,0:T(8,128)(2,1)} %momentum.1, ...), custom_call_target="tpu_custom_call" | custom-call | flops 2415919104 | bytes 9437184 | tf_op jit(solution)/shard_map/gather_near/load/pallas_call | solution.py:266
  13.5 1.6 %collective-permute-done.refs_1_ = bf16[256,1024]{1,0:T(8,128)(2,1)S(1)} collective-permute-done((bf16[256,1024]{1,0:T(8,128)(2,1)}, bf16[256,1024]{1,0:T(8,128)(2,1)S(1)}, u32[]{:S(2)}, u32[]{:S(2)}) %collective-permute-start) | collective-permute-done | bytes 524320 | tf_op jit(solution)/shard_map/gather_near/ppermute | solution.py:424
  15.2 1.2 %collective-permute-start.7 = (bf16[256,1024]{1,0:T(8,128)(2,1)S(1)}, bf16[256,1024]{1,0:T(8,128)(2,1)S(1)}, u32[]{:S(2)}, u32[]{:S(2)}) collective-permute-start(bf16[256,1024]{1,0:T(8,128)(2,1)S(1)} %collective-permute-done.refs_1_), channel_id=1, source_target_pairs={{0,1},{1,0},{2,3},{3,2},{4,5},{5,4},{6,7},{7,6},{8,9},{9,8},{10,11... | collective-permute-start | bytes 1572872 | tf_op jit(solution)/shard_map/gather_middle/ppermute | solution.py:421
  17.0 2.1 %collective-permute-done.3.refs_2_ = bf16[256,1024]{1,0:T(8,128)(2,1)S(1)} collective-permute-done((bf16[256,1024]{1,0:T(8,128)(2,1)}, bf16[256,1024]{1,0:T(8,128)(2,1)S(1)}, u32[]{:S(2)}, u32[]{:S(2)}) %collective-permute-start.3) | collective-permute-done | bytes 524320 | tf_op jit(solution)/shard_map/gather_near/ppermute | solution.py:427
  20.7 2.0 %collective-permute-start.9 = (bf16[128,1024]{1,0:T(8,128)(2,1)S(1)}, bf16[128,1024]{1,0:T(8,128)(2,1)S(1)}, u32[]{:S(2)}, u32[]{:S(2)}) collective-permute-start(bf16[128,1024]{1,0:T(8,128)(2,1)S(1)} %get-tuple-element.66), channel_id=1, source_target_pairs={{0,6},{2,0},{4,2},{6,4},{1,7},{3,1},{5,3},{7,5},{8,14},{10,8},{12,... | collective-permute-start | bytes 786440 | tf_op jit(solution)/shard_map/gather_middle/ppermute | solution.py:424
  22.6 3.0 %add.139.refs_5_ = f32[1024,1536]{1,0:T(8,128)} custom-call(s32[3]{0:T(128)S(1)} %get-tuple-element.44.places, bf16[256,1024]{1,0:T(8,128)(2,1)S(1)} %collective-permute-done.2.refs_0_, bf16[256,1024]{1,0:T(8,128)(2,1)S(1)} %collective-permute-done.refs_1_, bf16[256,1024]{1,0:T(8,128)(2,1)S(1)} %collective-permute-done.3.refs_2_, ...), custom_call_target="tpu_custom_call" | custom-call | flops 1207959552 | bytes 3145728 | tf_op jit(solution)/shard_map/add/pallas_call | solution.py:294
  25.7 1.2 %collective-permute-done.4.refs_2_ = bf16[128,1024]{1,0:T(8,128)(2,1)S(1)} collective-permute-done((bf16[128,1024]{1,0:T(8,128)(2,1)S(1)}, bf16[128,1024]{1,0:T(8,128)(2,1)S(1)}, u32[]{:S(2)}, u32[]{:S(2)}) %collective-permute-start.4) | collective-permute-done | bytes 262176 | tf_op jit(solution)/shard_map/gather_middle/ppermute | solution.py:427
  27.1 1.3 %tally.2.refs_6_ = f32[192,1024]{1,0:T(8,128)S(1)} custom-call(s32[3]{0:T(128)S(1)} %get-tuple-element.44.places, bf16[256,1024]{1,0:T(8,128)(2,1)S(1)} %collective-permute-done.2.refs_0_, bf16[256,1024]{1,0:T(8,128)(2,1)S(1)} %collective-permute-done.refs_1_, bf16[256,1024]{1,0:T(8,128)(2,1)S(1)} %collective-permute-done.3.refs_2_, ...), custom_call_target="tpu_custom_call" | custom-call | flops 603979776 | tf_op jit(solution)/shard_map/tally/pallas_call | solution.py:310
  28.5 3.1 %add.140.refs_8_ = f32[1024,1536]{1,0:T(8,128)} custom-call(s32[3]{0:T(128)S(1)} %get-tuple-element.44.places, bf16[256,1024]{1,0:T(8,128)(2,1)S(1)} %collective-permute-done.2.refs_0_, bf16[256,1024]{1,0:T(8,128)(2,1)S(1)} %collective-permute-done.refs_1_, bf16[256,1024]{1,0:T(8,128)(2,1)S(1)} %collective-permute-done.3.refs_2_, ...), custom_call_target="tpu_custom_call", output_to_operand_aliasing={{}: (6, {})} | custom-call | flops 1207959552 | bytes 3145728 | tf_op jit(solution)/shard_map/add/pallas_call | solution.py:294
  31.6 0.9 collective-permute-done.8.refs_1_
  32.5 1.3 %tally.3.refs_3_ = f32[192,1024]{1,0:T(8,128)S(1)} custom-call(s32[3]{0:T(128)S(1)} %get-tuple-element.51.places, bf16[256,1024]{1,0:T(8,128)(2,1)S(1)} %collective-permute-done.7.refs_0_, bf16[128,1024]{1,0:T(8,128)(2,1)S(1)} %collective-permute-done.8.refs_1_, bf16[128,1024]{1,0:T(8,128)(2,1)S(1)} %collective-permute-done.4.refs_2_, ...), custom_call_target="tpu_custom_call" | custom-call | flops 603979776 | tf_op jit(solution)/shard_map/tally/pallas_call | solution.py:310
  33.9 4.2 %collective-permute-done.6.refs_1_.refs_6_ = bf16[128,1024]{1,0:T(8,128)(2,1)S(1)} collective-permute-done((bf16[128,1024]{1,0:T(8,128)(2,1)S(1)}, bf16[128,1024]{1,0:T(8,128)(2,1)S(1)}, u32[]{:S(2)}, u32[]{:S(2)}) %collective-permute-start.6) | collective-permute-done | bytes 262176 | tf_op jit(solution)/shard_map/gather_far/ppermute | solution.py:427
  38.5 3.1 %collective-permute-start.10 = (f32[768,128]{1,0:T(8,128)S(1)}, f32[768,128]{1,0:T(8,128)S(1)}, u32[]{:S(2)}, u32[]{:S(2)}) collective-permute-start(f32[768,128]{1,0:T(8,128)S(1)} %get-tuple-element.56), channel_id=1, source_target_pairs={{0,8},{8,0},{1,9},{9,1},{2,10},{10,2},{3,11},{11,3},{4,12},{12,4},... | collective-permute-start | bytes 1179656 | tf_op jit(solution)/shard_map/sum_core/ppermute | solution.py:462
  41.6 1.3 %collective-permute-done.10.other = f32[768,128]{1,0:T(8,128)S(1)} collective-permute-done((f32[768,128]{1,0:T(8,128)S(1)}, f32[768,128]{1,0:T(8,128)S(1)}, u32[]{:S(2)}, u32[]{:S(2)}) %collective-permute-start.10) | collective-permute-done | bytes 393248 | tf_op jit(solution)/shard_map/sum_core/ppermute | solution.py:462
  42.9 1.1 %join.1 = (f32[768,128]{1,0:T(8,128)}, f32[192,1024]{1,0:T(8,128)}) custom-call(f32[768,128]{1,0:T(8,128)S(1)} %get-tuple-element.55.mine, f32[768,128]{1,0:T(8,128)S(1)} %collective-permute-done.10.other, f32[192,1024]{1,0:T(8,128)S(1)} %get-tuple-element.57.kept), custom_call_target="tpu_custom_call" | custom-call | tf_op jit(solution)/shard_map/sum_core/join/pallas_call | solution.py:362
  44.0 10.5 %all-to-all-start = ((f32[16,48,128]{2,1,0:T(8,128)}), f32[16,48,128]{2,1,0:T(8,128)S(1)}, u32[]{:S(2)}, u32[]{:S(2)}) async-start(f32[16,48,128]{2,1,0:T(8,128)} %bitcast.17), calls=%async_computation | async-start | bytes 786432 | tf_op jit(solution)/shard_map/sum_chips/all_to_all | solution.py:464
  54.5 9.3 %finish.1 = bf16[1,1024,1536]{2,1,0:T(8,128)(2,1)} custom-call(s32[4]{0:T(128)S(1)} %pad_add_fusion.2.places, bf16[256,1024]{1,0:T(8,128)(2,1)} %copy-done, bf16[128,1024]{1,0:T(8,128)(2,1)} %copy-done.4, bf16[128,1024]{1,0:T(8,128)(2,1)} %copy-done.2, bf16[128,1024]{1,0:T(8,128)(2,1)} %copy-done.1, bf16[128,1024]{1,0:T(8,128)(2,1)} %copy-done.3, ...), custom_call_target="tpu_custom_call" | custom-call | flops 6442450944 | bytes 9437184 | tf_op jit(solution)/shard_map/finish/pallas_call | solution.py:341
  63.9 5.6 %all-to-all-done = f32[16,48,128]{2,1,0:T(8,128)S(1)} async-done(((f32[16,48,128]{2,1,0:T(8,128)}), f32[16,48,128]{2,1,0:T(8,128)S(1)}, u32[]{:S(2)}, u32[]{:S(2)}) %all-to-all-start) | async-done | bytes 393248 | tf_op jit(solution)/shard_map/sum_chips/all_to_all | solution.py:464
  69.6 16.2 %all_to_all.23 = s16[16,64,128]{2,1,0:T(8,128)(2,1)S(1)} all-to-all(s16[16,64,128]{2,1,0:T(8,128)(2,1)S(1)} %bitcast.16), channel_id=1, replica_groups=mesh['z'=8,'xh'=2,'core'=2,'y'=4,'xl'=2] {'z','xh'}, dimensions={0} | all-to-all | bytes 524288 | tf_op jit(solution)/shard_map/spread_chips/all_to_all | solution.py:468
  85.8 2.2 %collective-permute-start.11 = (s16[1024,128]{1,0:T(8,128)(2,1)S(1)}, s16[1024,128]{1,0:T(8,128)(2,1)S(1)}, u32[]{:S(2)}, u32[]{:S(2)}) collective-permute-start(s16[1024,128]{1,0:T(8,128)(2,1)S(1)} %bitcast.14), channel_id=1, source_target_pairs={{0,8},{8,0},{1,9},{9,1},{2,10},{10,2},{3,11},{11,3},{4,12},{12,4},... | collective-permute-start | bytes 786440 | tf_op jit(solution)/shard_map/spread_core/ppermute | solution.py:470
  88.0 1.7 %update.2.refs_0_ = bf16[1024,1536]{1,0:T(8,128)(2,1)} custom-call(s32[1]{0:T(128)} %bitcast.8.core.where, s16[1024,128]{1,0:T(8,128)(2,1)S(1)} %bitcast.15, bf16[96,256]{1,0:T(8,128)(2,1)S(1)} %pad_maximum_fusion.refs_10_.stacked), custom_call_target="tpu_custom_call" | custom-call | flops 150994944 | bytes 1572864 | tf_op jit(solution)/shard_map/update/pallas_call | solution.py:386
  89.7 1.7 %update.3 = bf16[1024,1536]{1,0:T(8,128)(2,1)} custom-call(s32[1]{0:T(128)S(6)} %sub.7.where, s16[1024,128]{1,0:T(8,128)(2,1)S(1)} %collective-permute-done.11.whole, bf16[96,256]{1,0:T(8,128)(2,1)S(1)} %pad_maximum_fusion.refs_10_.stacked, bf16[1024,1536]{1,0:T(8,128)(2,1)} %update.2.refs_0_), custom_call_target="tpu_custom_call", output_to_operand_aliasing={{}: (3, {})} | custom-call | flops 150994944 | bytes 1572864 | tf_op jit(solution)/shard_map/update/pallas_call | solution.py:386
  (38 shorter events, 4.6 us)
Async XLA Ops:
  0.6 14.5 %collective-permute-start = (bf16[256,1024]{1,0:T(8,128)(2,1)}, bf16[256,1024]{1,0:T(8,128)(2,1)S(1)}, u32[]{:S(2)}, u32[]{:S(2)}) collective-permute-start(bf16[256,1024]{1,0:T(8,128)(2,1)} %x_rows.1), channel_id=1, source_target_pairs={{0,6},{2,0},{4,2},{6,4},{1,7},{3,1},{5,3},{7,5},{8,14},{10,8},{12,... | collective-permute-start | bytes 1572872 | tf_op jit(solution)/shard_map/gather_near/ppermute | solution.py:424
  4.3 12.7 %collective-permute-start.2 = (bf16[256,1024]{1,0:T(8,128)(2,1)}, bf16[256,1024]{1,0:T(8,128)(2,1)S(1)}, u32[]{:S(2)}, u32[]{:S(2)}) collective-permute-start(bf16[256,1024]{1,0:T(8,128)(2,1)} %x_rows.1), channel_id=1, source_target_pairs={{0,1},{1,0},{2,3},{3,2},{4,5},{5,4},{6,7},{7,6},{8,9},{9,8},{10,11... | collective-permute-start | bytes 1572872 | tf_op jit(solution)/shard_map/gather_near/ppermute | solution.py:421
  5.5 13.6 %collective-permute-start.3 = (bf16[256,1024]{1,0:T(8,128)(2,1)}, bf16[256,1024]{1,0:T(8,128)(2,1)S(1)}, u32[]{:S(2)}, u32[]{:S(2)}) collective-permute-start(bf16[256,1024]{1,0:T(8,128)(2,1)} %x_rows.1), channel_id=1, source_target_pairs={{0,2},{2,4},{4,6},{6,0},{1,3},{3,5},{5,7},{7,1},{8,10},{10,12},{12... | collective-permute-start | bytes 1572872 | tf_op jit(solution)/shard_map/gather_near/ppermute | solution.py:427
  15.2 17.3 %collective-permute-start.7 = (bf16[256,1024]{1,0:T(8,128)(2,1)S(1)}, bf16[256,1024]{1,0:T(8,128)(2,1)S(1)}, u32[]{:S(2)}, u32[]{:S(2)}) collective-permute-start(bf16[256,1024]{1,0:T(8,128)(2,1)S(1)} %collective-permute-done.refs_1_), channel_id=1, source_target_pairs={{0,1},{1,0},{2,3},{3,2},{4,5},{5,4},{6,7},{7,6},{8,9},{9,8},{10,11... | collective-permute-start | bytes 1572872 | tf_op jit(solution)/shard_map/gather_middle/ppermute | solution.py:421
  19.1 6.6 %collective-permute-start.1 = (bf16[128,1024]{1,0:T(8,128)(2,1)S(1)}, bf16[128,1024]{1,0:T(8,128)(2,1)S(1)}, u32[]{:S(2)}, u32[]{:S(2)}) collective-permute-start(bf16[128,1024]{1,0:T(8,128)(2,1)S(1)} %get-tuple-element.67), channel_id=1, source_target_pairs={{0,6},{2,0},{4,2},{6,4},{1,7},{3,1},{5,3},{7,5},{8,14},{10,8},{12,... | collective-permute-start | bytes 786440 | tf_op jit(solution)/shard_map/gather_middle/ppermute | solution.py:424
  19.9 7.0 %collective-permute-start.4 = (bf16[128,1024]{1,0:T(8,128)(2,1)S(1)}, bf16[128,1024]{1,0:T(8,128)(2,1)S(1)}, u32[]{:S(2)}, u32[]{:S(2)}) collective-permute-start(bf16[128,1024]{1,0:T(8,128)(2,1)S(1)} %get-tuple-element.69), channel_id=1, source_target_pairs={{0,2},{2,4},{4,6},{6,0},{1,3},{3,5},{5,7},{7,1},{8,10},{10,12},{12... | collective-permute-start | bytes 786440 | tf_op jit(solution)/shard_map/gather_middle/ppermute | solution.py:427
  20.7 10.9 %collective-permute-start.9 = (bf16[128,1024]{1,0:T(8,128)(2,1)S(1)}, bf16[128,1024]{1,0:T(8,128)(2,1)S(1)}, u32[]{:S(2)}, u32[]{:S(2)}) collective-permute-start(bf16[128,1024]{1,0:T(8,128)(2,1)S(1)} %get-tuple-element.66), channel_id=1, source_target_pairs={{0,6},{2,0},{4,2},{6,4},{1,7},{3,1},{5,3},{7,5},{8,14},{10,8},{12,... | collective-permute-start | bytes 786440 | tf_op jit(solution)/shard_map/gather_middle/ppermute | solution.py:424
  22.6 9.8 %collective-permute-start.8 = (bf16[128,1024]{1,0:T(8,128)(2,1)S(1)}, bf16[128,1024]{1,0:T(8,128)(2,1)S(1)}, u32[]{:S(2)}, u32[]{:S(2)}) collective-permute-start(bf16[128,1024]{1,0:T(8,128)(2,1)S(1)} %get-tuple-element.68), channel_id=1, source_target_pairs={{0,2},{2,4},{4,6},{6,0},{1,3},{3,5},{5,7},{7,1},{8,10},{10,12},{12... | collective-permute-start | bytes 786440 | tf_op jit(solution)/shard_map/gather_middle/ppermute | solution.py:427
  25.7 6.8 %copy-start.1 = (bf16[128,1024]{1,0:T(8,128)(2,1)}, bf16[128,1024]{1,0:T(8,128)(2,1)S(1)}, u32[]{:S(2)}) copy-start(bf16[128,1024]{1,0:T(8,128)(2,1)S(1)} %collective-permute-done.1.refs_3_) | copy-start | bytes 786436
  26.9 5.6 %copy-start.2 = (bf16[128,1024]{1,0:T(8,128)(2,1)}, bf16[128,1024]{1,0:T(8,128)(2,1)S(1)}, u32[]{:S(2)}) copy-start(bf16[128,1024]{1,0:T(8,128)(2,1)S(1)} %collective-permute-done.4.refs_2_) | copy-start | bytes 786436
  26.9 7.0 %collective-permute-start.5 = (bf16[128,1024]{1,0:T(8,128)(2,1)S(1)}, bf16[128,1024]{1,0:T(8,128)(2,1)S(1)}, u32[]{:S(2)}, u32[]{:S(2)}) collective-permute-start(bf16[128,1024]{1,0:T(8,128)(2,1)S(1)} %collective-permute-done.1.refs_3_), channel_id=1, source_target_pairs={{0,1},{1,0},{2,3},{3,2},{4,5},{5,4},{6,7},{7,6},{8,9},{9,8},{10,11... | collective-permute-start | bytes 786440 | tf_op jit(solution)/shard_map/gather_far/ppermute | solution.py:421
  27.1 11.0 %collective-permute-start.6 = (bf16[128,1024]{1,0:T(8,128)(2,1)S(1)}, bf16[128,1024]{1,0:T(8,128)(2,1)S(1)}, u32[]{:S(2)}, u32[]{:S(2)}) collective-permute-start(bf16[128,1024]{1,0:T(8,128)(2,1)S(1)} %collective-permute-done.4.refs_2_), channel_id=1, source_target_pairs={{0,2},{2,4},{4,6},{6,0},{1,3},{3,5},{5,7},{7,1},{8,10},{10,12},{12... | collective-permute-start | bytes 786440 | tf_op jit(solution)/shard_map/gather_far/ppermute | solution.py:427
  31.6 22.9 %copy-start.3 = (bf16[128,1024]{1,0:T(8,128)(2,1)}, bf16[128,1024]{1,0:T(8,128)(2,1)S(1)}, u32[]{:S(2)}) copy-start(bf16[128,1024]{1,0:T(8,128)(2,1)S(1)} %collective-permute-done.9.refs_4_) | copy-start | bytes 786436
  32.5 22.0 %copy-start.4 = (bf16[128,1024]{1,0:T(8,128)(2,1)}, bf16[128,1024]{1,0:T(8,128)(2,1)S(1)}, u32[]{:S(2)}) copy-start(bf16[128,1024]{1,0:T(8,128)(2,1)S(1)} %collective-permute-done.8.refs_1_) | copy-start | bytes 786436
  32.5 22.0 %copy-start = (bf16[256,1024]{1,0:T(8,128)(2,1)}, bf16[256,1024]{1,0:T(8,128)(2,1)S(1)}, u32[]{:S(2)}) copy-start(bf16[256,1024]{1,0:T(8,128)(2,1)S(1)} %collective-permute-done.7.refs_0_) | copy-start | bytes 1572868
  33.9 20.7 %copy-start.5 = (bf16[128,1024]{1,0:T(8,128)(2,1)}, bf16[128,1024]{1,0:T(8,128)(2,1)S(1)}, u32[]{:S(2)}) copy-start(bf16[128,1024]{1,0:T(8,128)(2,1)S(1)} %collective-permute-done.5.refs_0_.refs_5_) | copy-start | bytes 786436
  38.1 5.9 %copy-start.6 = (bf16[128,1024]{1,0:T(8,128)(2,1)}, bf16[128,1024]{1,0:T(8,128)(2,1)S(1)}, u32[]{:S(2)}) copy-start(bf16[128,1024]{1,0:T(8,128)(2,1)S(1)} %collective-permute-done.6.refs_1_.refs_6_) | copy-start | bytes 786436
  38.5 4.5 %collective-permute-start.10 = (f32[768,128]{1,0:T(8,128)S(1)}, f32[768,128]{1,0:T(8,128)S(1)}, u32[]{:S(2)}, u32[]{:S(2)}) collective-permute-start(f32[768,128]{1,0:T(8,128)S(1)} %get-tuple-element.56), channel_id=1, source_target_pairs={{0,8},{8,0},{1,9},{9,1},{2,10},{10,2},{3,11},{11,3},{4,12},{12,4},... | collective-permute-start | bytes 1179656 | tf_op jit(solution)/shard_map/sum_core/ppermute | solution.py:462
  44.0 25.5 %all-to-all-start = ((f32[16,48,128]{2,1,0:T(8,128)}), f32[16,48,128]{2,1,0:T(8,128)S(1)}, u32[]{:S(2)}, u32[]{:S(2)}) async-start(f32[16,48,128]{2,1,0:T(8,128)} %bitcast.17), calls=%async_computation | async-start | bytes 786432 | tf_op jit(solution)/shard_map/sum_chips/all_to_all | solution.py:464
  85.8 3.9 %collective-permute-start.11 = (s16[1024,128]{1,0:T(8,128)(2,1)S(1)}, s16[1024,128]{1,0:T(8,128)(2,1)S(1)}, u32[]{:S(2)}, u32[]{:S(2)}) collective-permute-start(s16[1024,128]{1,0:T(8,128)(2,1)S(1)} %bitcast.14), channel_id=1, source_target_pairs={{0,8},{8,0},{1,9},{9,1},{2,10},{10,2},{3,11},{11,3},{4,12},{12,4},... | collective-permute-start | bytes 786440 | tf_op jit(solution)/shard_map/spread_core/ppermute | solution.py:470

commit v3 on v2

--- a/solution.py
+++ b/solution.py
@@ -99,9 +99,8 @@
     half = coded.shape[0] // 2
     for s, pieces in enumerate(xs):
         x = take(pieces, columns)
-        tokens = tokens_of(places[s], x.shape[0])
-        value = value + (dot(coded[:half, tokens], x, (1, 0)) + dot(coded[half:, tokens], x, (1, 0)))
-    return value
+        value = value + dot(coded[:, tokens_of(places[s], x.shape[0])], x, (1, 0))
+    return value[:half] + value[half:]
 
 
 def grad_sum(places, xs, grad_in, rows, columns):
@@ -221,7 +220,7 @@
 
 
 def update_kernel(band, chips, where, whole, stacked, *refs):
-    update = refs[-1]
+    update, staged, sems = refs[-3:]
     rows = whole.shape[0] // chips - PAD
     values = []
     for i in range(chips):
@@ -230,11 +229,19 @@
         power = whole[start + rows : start + rows + PAD, :].astype(jnp.int32).astype(F32)[:1]
         values.append(level * jnp.exp2(power - 15.0))
     value = jnp.concatenate(values, axis=0)
-    tiles = update.shape[0] // 128
+    tiles = staged.shape[0] // 128
     kept = value.shape[0] // tiles
-    for b in range(update.shape[1] // GROUP):
-        parts = [value[t * kept + b * band : t * kept + (b + 1) * band] for t in range(tiles)]
-        update[:, block(b, GROUP)] = decode(jnp.concatenate(parts, axis=1), stacked[...]).astype(BF16)
+    span = pl.ds(pl.multiple_of(where[0] * staged.shape[0], staged.shape[0]), staged.shape[0])
+    outs = []
+    for w in range(staged.shape[1] // TILE):
+        for b in range(w * TILE // GROUP, (w + 1) * TILE // GROUP):
+            parts = [value[t * kept + b * band : t * kept + (b + 1) * band] for t in range(tiles)]
+            staged[:, block(b, GROUP)] = decode(jnp.concatenate(parts, axis=1), stacked[...]).astype(BF16)
+        wide = block(w, TILE)
+        outs.append(pltpu.make_async_copy(staged.at[:, wide], update.at[span, wide], sems.at[w]))
+        outs[-1].start()
+    for out in outs:
+        out.wait()
 
 
 VMEM = pl.BlockSpec(memory_space=pltpu.VMEM)
@@ -384,23 +391,16 @@
 def make_update(where, whole, stacked, band, rows, columns, update=None):
     others = [] if update is None else [update]
     return pl.pallas_call(
-        functools.partial(update_kernel, band, 8),
-        grid_spec=pltpu.PrefetchScalarGridSpec(
-            num_scalar_prefetch=1,
-            grid=(2,),
-            in_specs=[
-                pl.BlockSpec((whole.shape[0] // 2, whole.shape[1]), lambda i, where: (i, 0)),
-                pl.BlockSpec(stacked.shape, lambda i, where: (0, 0)),
-            ]
-            + [ANY] * len(others),
-            out_specs=pl.BlockSpec((rows // 4, columns), lambda i, where: (2 * where[0] + i, 0)),
-        ),
+        functools.partial(update_kernel, band, 16),
+        in_specs=[SMEM, VMEM, VMEM] + [ANY] * len(others),
+        out_specs=ANY,
         out_shape=jax.ShapeDtypeStruct((rows, columns), BF16),
         input_output_aliases={3: 0} if others else {},
+        scratch_shapes=[pltpu.VMEM((rows // 2, columns), BF16), pltpu.SemaphoreType.DMA((columns // TILE,))],
         compiler_params=params(16),
         cost_estimate=estimate(rows * columns * 96, rows * columns),
         name="update",
-    )(where, whole, stacked, *others)
+    )(where, held(whole), held(stacked), *others)
 
 
 def shards(x_rows, grad_out, momentum, band_index):

time: 91.6 us -> 91.4 us (level)
  transfers between devices with their start and end apart: 13 -> 13, of which waited for: 8 -> 8; matrix products, arithmetic and copies ran while one was open for 2% -> 2% of each run, Pallas kernels for 29% -> 28%
where the time goes in v3:
time: 91.4 us; the launch traced here: 91.2 us
  Pallas kernels  29 us (32%)
  starting transfers between devices  25.6 us (28%)
  waiting for transfers between devices  17.5 us (19%)
  blocking collectives  16.2 us (18%)
  other arithmetic  1.68 us (2%)
  between operations  1.02 us (1%)
    all_to_all x1, blocking collectives, shards(): whole = lax.all_to_all(sum_parts(parts, 16), ('z', 'xh'), 0, 0, tiled=True)  16.2 us
    all_to_all x1, starting transfers between devices, shards(): parts = lax.all_to_all(mine, ('z', 'xh'), 0, 0, tiled=True)  10.5 us
    pallas_call x1, Pallas kernels, finish(): pl.pallas_call(functools.partial(fresh_kernel, groups, band), in_specs=[S...  9.34 us
    ppermute x4, waiting for transfers between devices, from_below(): return lax.ppermute(v, 'y', ring(4, 1))  8.42 us
    ppermute x3, starting transfers between devices, from_above(): return lax.ppermute(v, 'y', ring(4, -1))  6.35 us
    pallas_call x1, Pallas kernels, load(): pl.pallas_call(functools.partial(load_kernel, band), in_specs=[SMEM, ANY,...  6.34 us
    pallas_call x2, Pallas kernels, add(): pl.pallas_call(functools.partial(add_kernel, groups, span), in_specs=[SME...  6.13 us
    all_to_all x1, waiting for transfers between devices, shards(): parts = lax.all_to_all(mine, ('z', 'xh'), 0, 0, tiled=True)  5.6 us
  transfers between devices with their start and end apart: 13, of which 8 were waited for; matrix products, arithmetic and copies ran while one was open for 2% of the time, Pallas kernels for 28%

profile of v3, /device:TPU:1, one launch (start us, length us, event | category | flops | bytes accessed | tf_op | source)
XLA Modules:
  0.0 91.2 jit_solution(1200398496992670468)
XLA Ops:
  0.6 3.6 %collective-permute-start = (bf16[256,1024]{1,0:T(8,128)(2,1)}, bf16[256,1024]{1,0:T(8,128)(2,1)S(1)}, u32[]{:S(2)}, u32[]{:S(2)}) collective-permute-start(bf16[256,1024]{1,0:T(8,128)(2,1)} %x_rows.1), channel_id=1, source_target_pairs={{0,6},{2,0},{4,2},{6,4},{1,7},{3,1},{5,3},{7,5},{8,14},{10,8},{12,... | collective-permute-start | bytes 1572872 | tf_op jit(solution)/shard_map/gather_near/ppermute | solution.py:424
  4.3 1.2 %collective-permute-start.2 = (bf16[256,1024]{1,0:T(8,128)(2,1)}, bf16[256,1024]{1,0:T(8,128)(2,1)S(1)}, u32[]{:S(2)}, u32[]{:S(2)}) collective-permute-start(bf16[256,1024]{1,0:T(8,128)(2,1)} %x_rows.1), channel_id=1, source_target_pairs={{0,1},{1,0},{2,3},{3,2},{4,5},{5,4},{6,7},{7,6},{8,9},{9,8},{10,11... | collective-permute-start | bytes 1572872 | tf_op jit(solution)/shard_map/gather_near/ppermute | solution.py:421
  7.2 6.3 %load.1 = (bf16[384,2048]{1,0:T(8,128)(2,1)S(1)}, f32[192,1024]{1,0:T(8,128)S(1)}, bf16[256,1024]{1,0:T(8,128)(2,1)}, bf16[2048,1536]{1,0:T(8,128)(2,1)S(1)}, f32[1024,1536]{1,0:T(8,128)S(1)}) custom-call(s32[1]{0:T(128)} %bitcast.place, bf16[2048,1536]{1,0:T(8,128)(2,1)} %refs_7_.1, bf16[1,1024,1536]{2,1,0:T(8,128)(2,1)} %momentum.1, ...), custom_call_target="tpu_custom_call" | custom-call | flops 2415919104 | bytes 9437184 | tf_op jit(solution)/shard_map/gather_near/load/pallas_call | solution.py:273
  13.5 1.6 %collective-permute-done.refs_1_ = bf16[256,1024]{1,0:T(8,128)(2,1)S(1)} collective-permute-done((bf16[256,1024]{1,0:T(8,128)(2,1)}, bf16[256,1024]{1,0:T(8,128)(2,1)S(1)}, u32[]{:S(2)}, u32[]{:S(2)}) %collective-permute-start) | collective-permute-done | bytes 524320 | tf_op jit(solution)/shard_map/gather_near/ppermute | solution.py:424
  15.2 1.2 %collective-permute-start.7 = (bf16[256,1024]{1,0:T(8,128)(2,1)S(1)}, bf16[256,1024]{1,0:T(8,128)(2,1)S(1)}, u32[]{:S(2)}, u32[]{:S(2)}) collective-permute-start(bf16[256,1024]{1,0:T(8,128)(2,1)S(1)} %collective-permute-done.refs_1_), channel_id=1, source_target_pairs={{0,1},{1,0},{2,3},{3,2},{4,5},{5,4},{6,7},{7,6},{8,9},{9,8},{10,11... | collective-permute-start | bytes 1572872 | tf_op jit(solution)/shard_map/gather_middle/ppermute | solution.py:421
  17.0 2.1 %collective-permute-done.3.refs_2_ = bf16[256,1024]{1,0:T(8,128)(2,1)S(1)} collective-permute-done((bf16[256,1024]{1,0:T(8,128)(2,1)}, bf16[256,1024]{1,0:T(8,128)(2,1)S(1)}, u32[]{:S(2)}, u32[]{:S(2)}) %collective-permute-start.3) | collective-permute-done | bytes 524320 | tf_op jit(solution)/shard_map/gather_near/ppermute | solution.py:427
  20.7 2.0 %collective-permute-start.9 = (bf16[128,1024]{1,0:T(8,128)(2,1)S(1)}, bf16[128,1024]{1,0:T(8,128)(2,1)S(1)}, u32[]{:S(2)}, u32[]{:S(2)}) collective-permute-start(bf16[128,1024]{1,0:T(8,128)(2,1)S(1)} %get-tuple-element.66), channel_id=1, source_target_pairs={{0,6},{2,0},{4,2},{6,4},{1,7},{3,1},{5,3},{7,5},{8,14},{10,8},{12,... | collective-permute-start | bytes 786440 | tf_op jit(solution)/shard_map/gather_middle/ppermute | solution.py:424
  22.6 3.0 %add.139.refs_5_ = f32[1024,1536]{1,0:T(8,128)} custom-call(s32[3]{0:T(128)S(1)} %get-tuple-element.44.places, bf16[256,1024]{1,0:T(8,128)(2,1)S(1)} %collective-permute-done.2.refs_0_, bf16[256,1024]{1,0:T(8,128)(2,1)S(1)} %collective-permute-done.refs_1_, bf16[256,1024]{1,0:T(8,128)(2,1)S(1)} %collective-permute-done.3.refs_2_, ...), custom_call_target="tpu_custom_call" | custom-call | flops 1207959552 | bytes 3145728 | tf_op jit(solution)/shard_map/add/pallas_call | solution.py:301
  25.7 1.2 %collective-permute-done.4.refs_2_ = bf16[128,1024]{1,0:T(8,128)(2,1)S(1)} collective-permute-done((bf16[128,1024]{1,0:T(8,128)(2,1)S(1)}, bf16[128,1024]{1,0:T(8,128)(2,1)S(1)}, u32[]{:S(2)}, u32[]{:S(2)}) %collective-permute-start.4) | collective-permute-done | bytes 262176 | tf_op jit(solution)/shard_map/gather_middle/ppermute | solution.py:427
  27.1 1.3 %tally.2.refs_6_ = f32[192,1024]{1,0:T(8,128)S(1)} custom-call(s32[3]{0:T(128)S(1)} %get-tuple-element.44.places, bf16[256,1024]{1,0:T(8,128)(2,1)S(1)} %collective-permute-done.2.refs_0_, bf16[256,1024]{1,0:T(8,128)(2,1)S(1)} %collective-permute-done.refs_1_, bf16[256,1024]{1,0:T(8,128)(2,1)S(1)} %collective-permute-done.3.refs_2_, ...), custom_call_target="tpu_custom_call" | custom-call | flops 603979776 | tf_op jit(solution)/shard_map/tally/pallas_call | solution.py:317
  28.4 3.1 %add.140.refs_8_ = f32[1024,1536]{1,0:T(8,128)} custom-call(s32[3]{0:T(128)S(1)} %get-tuple-element.44.places, bf16[256,1024]{1,0:T(8,128)(2,1)S(1)} %collective-permute-done.2.refs_0_, bf16[256,1024]{1,0:T(8,128)(2,1)S(1)} %collective-permute-done.refs_1_, bf16[256,1024]{1,0:T(8,128)(2,1)S(1)} %collective-permute-done.3.refs_2_, ...), custom_call_target="tpu_custom_call", output_to_operand_aliasing={{}: (6, {})} | custom-call | flops 1207959552 | bytes 3145728 | tf_op jit(solution)/shard_map/add/pallas_call | solution.py:301
  31.6 0.9 collective-permute-done.8.refs_1_
  32.5 1.3 %tally.3.refs_3_ = f32[192,1024]{1,0:T(8,128)S(1)} custom-call(s32[3]{0:T(128)S(1)} %get-tuple-element.51.places, bf16[256,1024]{1,0:T(8,128)(2,1)S(1)} %collective-permute-done.7.refs_0_, bf16[128,1024]{1,0:T(8,128)(2,1)S(1)} %collective-permute-done.8.refs_1_, bf16[128,1024]{1,0:T(8,128)(2,1)S(1)} %collective-permute-done.4.refs_2_, ...), custom_call_target="tpu_custom_call" | custom-call | flops 603979776 | tf_op jit(solution)/shard_map/tally/pallas_call | solution.py:317
  33.9 4.2 %collective-permute-done.6.refs_1_.refs_6_ = bf16[128,1024]{1,0:T(8,128)(2,1)S(1)} collective-permute-done((bf16[128,1024]{1,0:T(8,128)(2,1)S(1)}, bf16[128,1024]{1,0:T(8,128)(2,1)S(1)}, u32[]{:S(2)}, u32[]{:S(2)}) %collective-permute-start.6) | collective-permute-done | bytes 262176 | tf_op jit(solution)/shard_map/gather_far/ppermute | solution.py:427
  38.5 3.1 %collective-permute-start.10 = (f32[768,128]{1,0:T(8,128)S(1)}, f32[768,128]{1,0:T(8,128)S(1)}, u32[]{:S(2)}, u32[]{:S(2)}) collective-permute-start(f32[768,128]{1,0:T(8,128)S(1)} %get-tuple-element.56), channel_id=1, source_target_pairs={{0,8},{8,0},{1,9},{9,1},{2,10},{10,2},{3,11},{11,3},{4,12},{12,4},... | collective-permute-start | bytes 1179656 | tf_op jit(solution)/shard_map/sum_core/ppermute | solution.py:462
  41.6 1.3 %collective-permute-done.10.other = f32[768,128]{1,0:T(8,128)S(1)} collective-permute-done((f32[768,128]{1,0:T(8,128)S(1)}, f32[768,128]{1,0:T(8,128)S(1)}, u32[]{:S(2)}, u32[]{:S(2)}) %collective-permute-start.10) | collective-permute-done | bytes 393248 | tf_op jit(solution)/shard_map/sum_core/ppermute | solution.py:462
  42.9 1.1 %join.1 = (f32[768,128]{1,0:T(8,128)}, f32[192,1024]{1,0:T(8,128)}) custom-call(f32[768,128]{1,0:T(8,128)S(1)} %get-tuple-element.55.mine, f32[768,128]{1,0:T(8,128)S(1)} %collective-permute-done.10.other, f32[192,1024]{1,0:T(8,128)S(1)} %get-tuple-element.57.kept), custom_call_target="tpu_custom_call" | custom-call | tf_op jit(solution)/shard_map/sum_core/join/pallas_call | solution.py:369
  44.0 10.5 %all-to-all-start = ((f32[16,48,128]{2,1,0:T(8,128)}), f32[16,48,128]{2,1,0:T(8,128)S(1)}, u32[]{:S(2)}, u32[]{:S(2)}) async-start(f32[16,48,128]{2,1,0:T(8,128)} %bitcast.17), calls=%async_computation | async-start | bytes 786432 | tf_op jit(solution)/shard_map/sum_chips/all_to_all | solution.py:464
  54.5 9.3 %finish.1 = bf16[1,1024,1536]{2,1,0:T(8,128)(2,1)} custom-call(s32[4]{0:T(128)S(1)} %pad_add_fusion.2.places, bf16[256,1024]{1,0:T(8,128)(2,1)} %copy-done, bf16[128,1024]{1,0:T(8,128)(2,1)} %copy-done.4, bf16[128,1024]{1,0:T(8,128)(2,1)} %copy-done.2, bf16[128,1024]{1,0:T(8,128)(2,1)} %copy-done.1, bf16[128,1024]{1,0:T(8,128)(2,1)} %copy-done.3, ...), custom_call_target="tpu_custom_call" | custom-call | flops 6442450944 | bytes 9437184 | tf_op jit(solution)/shard_map/finish/pallas_call | solution.py:348
  63.9 5.6 %all-to-all-done = f32[16,48,128]{2,1,0:T(8,128)S(1)} async-done(((f32[16,48,128]{2,1,0:T(8,128)}), f32[16,48,128]{2,1,0:T(8,128)S(1)}, u32[]{:S(2)}, u32[]{:S(2)}) %all-to-all-start) | async-done | bytes 393248 | tf_op jit(solution)/shard_map/sum_chips/all_to_all | solution.py:464
  69.6 16.2 %all_to_all.23 = s16[16,64,128]{2,1,0:T(8,128)(2,1)S(1)} all-to-all(s16[16,64,128]{2,1,0:T(8,128)(2,1)S(1)} %bitcast.16), channel_id=1, replica_groups=mesh['z'=8,'xh'=2,'core'=2,'y'=4,'xl'=2] {'z','xh'}, dimensions={0} | all-to-all | bytes 524288 | tf_op jit(solution)/shard_map/spread_chips/all_to_all | solution.py:468
  85.8 2.2 %collective-permute-start.11 = (s16[1024,128]{1,0:T(8,128)(2,1)S(1)}, s16[1024,128]{1,0:T(8,128)(2,1)S(1)}, u32[]{:S(2)}, u32[]{:S(2)}) collective-permute-start(s16[1024,128]{1,0:T(8,128)(2,1)S(1)} %bitcast.14), channel_id=1, source_target_pairs={{0,8},{8,0},{1,9},{9,1},{2,10},{10,2},{3,11},{11,3},{4,12},{12,4},... | collective-permute-start | bytes 786440 | tf_op jit(solution)/shard_map/spread_core/ppermute | solution.py:470
  88.0 1.5 %update.2.refs_0_ = bf16[1024,1536]{1,0:T(8,128)(2,1)} custom-call(s32[1]{0:T(128)} %bitcast.8.core.where, s16[1024,128]{1,0:T(8,128)(2,1)S(1)} %bitcast.15, bf16[96,256]{1,0:T(8,128)(2,1)S(1)} %pad_maximum_fusion.refs_10_.stacked), custom_call_target="tpu_custom_call" | custom-call | flops 150994944 | bytes 1572864 | tf_op jit(solution)/shard_map/update/pallas_call | solution.py:393
  89.5 1.5 %update.3 = bf16[1024,1536]{1,0:T(8,128)(2,1)} custom-call(s32[1]{0:T(128)S(6)} %sub.7.where, s16[1024,128]{1,0:T(8,128)(2,1)S(1)} %collective-permute-done.11.whole, bf16[96,256]{1,0:T(8,128)(2,1)S(1)} %pad_maximum_fusion.refs_10_.stacked, bf16[1024,1536]{1,0:T(8,128)(2,1)} %update.2.refs_0_), custom_call_target="tpu_custom_call", output_to_operand_aliasing={{}: (3, {})} | custom-call | flops 150994944 | bytes 1572864 | tf_op jit(solution)/shard_map/update/pallas_call | solution.py:393
  (38 shorter events, 4.6 us)
Async XLA Ops:
  0.6 14.5 %collective-permute-start = (bf16[256,1024]{1,0:T(8,128)(2,1)}, bf16[256,1024]{1,0:T(8,128)(2,1)S(1)}, u32[]{:S(2)}, u32[]{:S(2)}) collective-permute-start(bf16[256,1024]{1,0:T(8,128)(2,1)} %x_rows.1), channel_id=1, source_target_pairs={{0,6},{2,0},{4,2},{6,4},{1,7},{3,1},{5,3},{7,5},{8,14},{10,8},{12,... | collective-permute-start | bytes 1572872 | tf_op jit(solution)/shard_map/gather_near/ppermute | solution.py:424
  4.3 12.7 %collective-permute-start.2 = (bf16[256,1024]{1,0:T(8,128)(2,1)}, bf16[256,1024]{1,0:T(8,128)(2,1)S(1)}, u32[]{:S(2)}, u32[]{:S(2)}) collective-permute-start(bf16[256,1024]{1,0:T(8,128)(2,1)} %x_rows.1), channel_id=1, source_target_pairs={{0,1},{1,0},{2,3},{3,2},{4,5},{5,4},{6,7},{7,6},{8,9},{9,8},{10,11... | collective-permute-start | bytes 1572872 | tf_op jit(solution)/shard_map/gather_near/ppermute | solution.py:421
  5.5 13.6 %collective-permute-start.3 = (bf16[256,1024]{1,0:T(8,128)(2,1)}, bf16[256,1024]{1,0:T(8,128)(2,1)S(1)}, u32[]{:S(2)}, u32[]{:S(2)}) collective-permute-start(bf16[256,1024]{1,0:T(8,128)(2,1)} %x_rows.1), channel_id=1, source_target_pairs={{0,2},{2,4},{4,6},{6,0},{1,3},{3,5},{5,7},{7,1},{8,10},{10,12},{12... | collective-permute-start | bytes 1572872 | tf_op jit(solution)/shard_map/gather_near/ppermute | solution.py:427
  15.2 17.3 %collective-permute-start.7 = (bf16[256,1024]{1,0:T(8,128)(2,1)S(1)}, bf16[256,1024]{1,0:T(8,128)(2,1)S(1)}, u32[]{:S(2)}, u32[]{:S(2)}) collective-permute-start(bf16[256,1024]{1,0:T(8,128)(2,1)S(1)} %collective-permute-done.refs_1_), channel_id=1, source_target_pairs={{0,1},{1,0},{2,3},{3,2},{4,5},{5,4},{6,7},{7,6},{8,9},{9,8},{10,11... | collective-permute-start | bytes 1572872 | tf_op jit(solution)/shard_map/gather_middle/ppermute | solution.py:421
  19.1 6.6 %collective-permute-start.1 = (bf16[128,1024]{1,0:T(8,128)(2,1)S(1)}, bf16[128,1024]{1,0:T(8,128)(2,1)S(1)}, u32[]{:S(2)}, u32[]{:S(2)}) collective-permute-start(bf16[128,1024]{1,0:T(8,128)(2,1)S(1)} %get-tuple-element.67), channel_id=1, source_target_pairs={{0,6},{2,0},{4,2},{6,4},{1,7},{3,1},{5,3},{7,5},{8,14},{10,8},{12,... | collective-permute-start | bytes 786440 | tf_op jit(solution)/shard_map/gather_middle/ppermute | solution.py:424
  19.9 7.0 %collective-permute-start.4 = (bf16[128,1024]{1,0:T(8,128)(2,1)S(1)}, bf16[128,1024]{1,0:T(8,128)(2,1)S(1)}, u32[]{:S(2)}, u32[]{:S(2)}) collective-permute-start(bf16[128,1024]{1,0:T(8,128)(2,1)S(1)} %get-tuple-element.69), channel_id=1, source_target_pairs={{0,2},{2,4},{4,6},{6,0},{1,3},{3,5},{5,7},{7,1},{8,10},{10,12},{12... | collective-permute-start | bytes 786440 | tf_op jit(solution)/shard_map/gather_middle/ppermute | solution.py:427
  20.7 10.9 %collective-permute-start.9 = (bf16[128,1024]{1,0:T(8,128)(2,1)S(1)}, bf16[128,1024]{1,0:T(8,128)(2,1)S(1)}, u32[]{:S(2)}, u32[]{:S(2)}) collective-permute-start(bf16[128,1024]{1,0:T(8,128)(2,1)S(1)} %get-tuple-element.66), channel_id=1, source_target_pairs={{0,6},{2,0},{4,2},{6,4},{1,7},{3,1},{5,3},{7,5},{8,14},{10,8},{12,... | collective-permute-start | bytes 786440 | tf_op jit(solution)/shard_map/gather_middle/ppermute | solution.py:424
  22.6 9.8 %collective-permute-start.8 = (bf16[128,1024]{1,0:T(8,128)(2,1)S(1)}, bf16[128,1024]{1,0:T(8,128)(2,1)S(1)}, u32[]{:S(2)}, u32[]{:S(2)}) collective-permute-start(bf16[128,1024]{1,0:T(8,128)(2,1)S(1)} %get-tuple-element.68), channel_id=1, source_target_pairs={{0,2},{2,4},{4,6},{6,0},{1,3},{3,5},{5,7},{7,1},{8,10},{10,12},{12... | collective-permute-start | bytes 786440 | tf_op jit(solution)/shard_map/gather_middle/ppermute | solution.py:427
  25.7 6.8 %copy-start.1 = (bf16[128,1024]{1,0:T(8,128)(2,1)}, bf16[128,1024]{1,0:T(8,128)(2,1)S(1)}, u32[]{:S(2)}) copy-start(bf16[128,1024]{1,0:T(8,128)(2,1)S(1)} %collective-permute-done.1.refs_3_) | copy-start | bytes 786436
  26.9 5.6 %copy-start.2 = (bf16[128,1024]{1,0:T(8,128)(2,1)}, bf16[128,1024]{1,0:T(8,128)(2,1)S(1)}, u32[]{:S(2)}) copy-start(bf16[128,1024]{1,0:T(8,128)(2,1)S(1)} %collective-permute-done.4.refs_2_) | copy-start | bytes 786436
  26.9 7.0 %collective-permute-start.5 = (bf16[128,1024]{1,0:T(8,128)(2,1)S(1)}, bf16[128,1024]{1,0:T(8,128)(2,1)S(1)}, u32[]{:S(2)}, u32[]{:S(2)}) collective-permute-start(bf16[128,1024]{1,0:T(8,128)(2,1)S(1)} %collective-permute-done.1.refs_3_), channel_id=1, source_target_pairs={{0,1},{1,0},{2,3},{3,2},{4,5},{5,4},{6,7},{7,6},{8,9},{9,8},{10,11... | collective-permute-start | bytes 786440 | tf_op jit(solution)/shard_map/gather_far/ppermute | solution.py:421
  27.1 11.0 %collective-permute-start.6 = (bf16[128,1024]{1,0:T(8,128)(2,1)S(1)}, bf16[128,1024]{1,0:T(8,128)(2,1)S(1)}, u32[]{:S(2)}, u32[]{:S(2)}) collective-permute-start(bf16[128,1024]{1,0:T(8,128)(2,1)S(1)} %collective-permute-done.4.refs_2_), channel_id=1, source_target_pairs={{0,2},{2,4},{4,6},{6,0},{1,3},{3,5},{5,7},{7,1},{8,10},{10,12},{12... | collective-permute-start | bytes 786440 | tf_op jit(solution)/shard_map/gather_far/ppermute | solution.py:427
  31.6 22.9 %copy-start.3 = (bf16[128,1024]{1,0:T(8,128)(2,1)}, bf16[128,1024]{1,0:T(8,128)(2,1)S(1)}, u32[]{:S(2)}) copy-start(bf16[128,1024]{1,0:T(8,128)(2,1)S(1)} %collective-permute-done.9.refs_4_) | copy-start | bytes 786436
  32.5 22.0 %copy-start.4 = (bf16[128,1024]{1,0:T(8,128)(2,1)}, bf16[128,1024]{1,0:T(8,128)(2,1)S(1)}, u32[]{:S(2)}) copy-start(bf16[128,1024]{1,0:T(8,128)(2,1)S(1)} %collective-permute-done.8.refs_1_) | copy-start | bytes 786436
  32.5 22.0 %copy-start = (bf16[256,1024]{1,0:T(8,128)(2,1)}, bf16[256,1024]{1,0:T(8,128)(2,1)S(1)}, u32[]{:S(2)}) copy-start(bf16[256,1024]{1,0:T(8,128)(2,1)S(1)} %collective-permute-done.7.refs_0_) | copy-start | bytes 1572868
  33.8 20.7 %copy-start.5 = (bf16[128,1024]{1,0:T(8,128)(2,1)}, bf16[128,1024]{1,0:T(8,128)(2,1)S(1)}, u32[]{:S(2)}) copy-start(bf16[128,1024]{1,0:T(8,128)(2,1)S(1)} %collective-permute-done.5.refs_0_.refs_5_) | copy-start | bytes 786436
  38.1 5.9 %copy-start.6 = (bf16[128,1024]{1,0:T(8,128)(2,1)}, bf16[128,1024]{1,0:T(8,128)(2,1)S(1)}, u32[]{:S(2)}) copy-start(bf16[128,1024]{1,0:T(8,128)(2,1)S(1)} %collective-permute-done.6.refs_1_.refs_6_) | copy-start | bytes 786436
  38.5 4.5 %collective-permute-start.10 = (f32[768,128]{1,0:T(8,128)S(1)}, f32[768,128]{1,0:T(8,128)S(1)}, u32[]{:S(2)}, u32[]{:S(2)}) collective-permute-start(f32[768,128]{1,0:T(8,128)S(1)} %get-tuple-element.56), channel_id=1, source_target_pairs={{0,8},{8,0},{1,9},{9,1},{2,10},{10,2},{3,11},{11,3},{4,12},{12,4},... | collective-permute-start | bytes 1179656 | tf_op jit(solution)/shard_map/sum_core/ppermute | solution.py:462
  44.0 25.5 %all-to-all-start = ((f32[16,48,128]{2,1,0:T(8,128)}), f32[16,48,128]{2,1,0:T(8,128)S(1)}, u32[]{:S(2)}, u32[]{:S(2)}) async-start(f32[16,48,128]{2,1,0:T(8,128)} %bitcast.17), calls=%async_computation | async-start | bytes 786432 | tf_op jit(solution)/shard_map/sum_chips/all_to_all | solution.py:464
  85.8 3.7 %collective-permute-start.11 = (s16[1024,128]{1,0:T(8,128)(2,1)S(1)}, s16[1024,128]{1,0:T(8,128)(2,1)S(1)}, u32[]{:S(2)}, u32[]{:S(2)}) collective-permute-start(s16[1024,128]{1,0:T(8,128)(2,1)S(1)} %bitcast.14), channel_id=1, source_target_pairs={{0,8},{8,0},{1,9},{9,1},{2,10},{10,2},{3,11},{11,3},{4,12},{12,4},... | collective-permute-start | bytes 786440 | tf_op jit(solution)/shard_map/spread_core/ppermute | solution.py:470

commit v4 on v3

--- a/solution.py
+++ b/solution.py
@@ -193,14 +193,21 @@
         out.wait()
 
 
-def join_kernel(mine, other, kept, out, kept_out, staged, sems):
-    save = pltpu.make_async_copy(kept, kept_out, sems.at[0])
-    staged[...] = mine[...] + other[...]
-    give = pltpu.make_async_copy(staged, out, sems.at[1])
-    give.start()
-    save.start()
-    give.wait()
-    save.wait()
+def save_kernel(kept, kept_out, sem):
+    copy = pltpu.make_async_copy(kept, kept_out, sem)
+    copy.start()
+    copy.wait()
+
+
+def join_kernel(mine, other, out, staged, sems):
+    halves = [block(h, mine.shape[0] // 2) for h in range(2)]
+    copies = []
+    for h, half in enumerate(halves):
+        staged[half, :] = mine[half, :] + other[half, :]
+        copies.append(pltpu.make_async_copy(staged.at[half], out.at[half], sems.at[h]))
+        copies[-1].start()
+    for copy in copies:
+        copy.wait()
 
 
 def part_kernel(chips, parts, spread):
@@ -365,16 +372,29 @@
     )(places, *map(far, xs), far(grad_out), far(total), far(kept), stacked)
 
 
-def join(mine, other, kept):
+def save(kept):
+    return pl.pallas_call(
+        save_kernel,
+        in_specs=[VMEM],
+        out_specs=ANY,
+        out_shape=pltpu.HBM(kept.shape, F32),
+        scratch_shapes=[pltpu.SemaphoreType.DMA],
+        compiler_params=params(4),
+        cost_estimate=estimate(0, kept.size * 4),
+        name="save",
+    )(held(kept))
+
+
+def join(mine, other):
     return pl.pallas_call(
         join_kernel,
-        in_specs=[VMEM] * 3,
-        out_specs=[ANY] * 2,
-        out_shape=[pltpu.HBM(mine.shape, F32), pltpu.HBM(kept.shape, F32)],
+        in_specs=[VMEM] * 2,
+        out_specs=ANY,
+        out_shape=pltpu.HBM(mine.shape, F32),
         scratch_shapes=[pltpu.VMEM(mine.shape, F32), pltpu.SemaphoreType.DMA((2,))],
         compiler_params=params(4),
         name="join",
-    )(held(mine), held(other), held(kept))
+    )(held(mine), held(other))
 
 
 def sum_parts(parts, chips):
@@ -450,7 +470,7 @@
     rows = momentum.shape[1]
     close = [[xn], [yp], [ym]]
     total = add(slice(0, rows // 2), near, close, grad_in, base)
-    y2[0], xym[1], total = lax.optimization_barrier((y2[0], xym[1], total))
+    y2[0], total = lax.optimization_barrier((y2[0], total))
     with jax.named_scope("gather_far"):
         xy2 = [across(y2[0]), from_below(xym[1])]
     total = add(slice(rows // 2, rows), near, close, grad_in, base, total)
@@ -459,7 +479,8 @@
     kept, total = lax.optimization_barrier((kept, total))
     kept, mine, other = code(last, core, [xy2], coded, kept)
     with jax.named_scope("sum_core"):
-        mine, kept = join(mine, lax.ppermute(other, "core", PAIR), kept)
+        other, kept = lax.optimization_barrier((lax.ppermute(other, "core", PAIR), save(kept)))
+        mine = join(mine, other)
     with jax.named_scope("sum_chips"):
         parts = lax.all_to_all(mine, ("z", "xh"), 0, 0, tiled=True)
     fresh = finish(ends, [[xyp], xym, y2, xy2], grad_out, total, kept, stacked, band)

time: 91.4 us -> 91.1 us (level)
  transfers between devices with their start and end apart: 13 -> 13, of which waited for: 8 -> 8; matrix products, arithmetic and copies ran while one was open for 2% -> 2% of each run, Pallas kernels for 28% -> 30%
where the time goes in v4:
time: 91.1 us; the launch traced here: 90.9 us
  Pallas kernels  29.6 us (32%)
  starting transfers between devices  25.7 us (28%)
  waiting for transfers between devices  16.6 us (18%)
  blocking collectives  16.2 us (18%)
  other arithmetic  1.68 us (2%)
  between operations  1.03 us (1%)
    all_to_all x1, blocking collectives, shards(): whole = lax.all_to_all(sum_parts(parts, 16), ('z', 'xh'), 0, 0, tiled=True)  16.2 us
    all_to_all x1, starting transfers between devices, shards(): parts = lax.all_to_all(mine, ('z', 'xh'), 0, 0, tiled=True)  10.5 us
    pallas_call x1, Pallas kernels, finish(): pl.pallas_call(functools.partial(fresh_kernel, groups, band), in_specs=[S...  9.34 us
    ppermute x4, waiting for transfers between devices, from_below(): return lax.ppermute(v, 'y', ring(4, 1))  8.33 us
    ppermute x3, starting transfers between devices, from_above(): return lax.ppermute(v, 'y', ring(4, -1))  6.35 us
    pallas_call x1, Pallas kernels, load(): pl.pallas_call(functools.partial(load_kernel, band), in_specs=[SMEM, ANY,...  6.34 us
    pallas_call x2, Pallas kernels, add(): pl.pallas_call(functools.partial(add_kernel, groups, span), in_specs=[SME...  6.13 us
    all_to_all x1, waiting for transfers between devices, shards(): parts = lax.all_to_all(mine, ('z', 'xh'), 0, 0, tiled=True)  5.6 us
  transfers between devices with their start and end apart: 13, of which 8 were waited for; matrix products, arithmetic and copies ran while one was open for 2% of the time, Pallas kernels for 30%

profile of v4, /device:TPU:1, one launch (start us, length us, event | category | flops | bytes accessed | tf_op | source)
XLA Modules:
  0.0 90.9 jit_solution(2475384984792080294)
XLA Ops:
  0.6 3.6 %collective-permute-start = (bf16[256,1024]{1,0:T(8,128)(2,1)}, bf16[256,1024]{1,0:T(8,128)(2,1)S(1)}, u32[]{:S(2)}, u32[]{:S(2)}) collective-permute-start(bf16[256,1024]{1,0:T(8,128)(2,1)} %x_rows.1), channel_id=1, source_target_pairs={{0,6},{2,0},{4,2},{6,4},{1,7},{3,1},{5,3},{7,5},{8,14},{10,8},{12,... | collective-permute-start | bytes 1572872 | tf_op jit(solution)/shard_map/gather_near/ppermute | solution.py:444
  4.3 1.2 %collective-permute-start.2 = (bf16[256,1024]{1,0:T(8,128)(2,1)}, bf16[256,1024]{1,0:T(8,128)(2,1)S(1)}, u32[]{:S(2)}, u32[]{:S(2)}) collective-permute-start(bf16[256,1024]{1,0:T(8,128)(2,1)} %x_rows.1), channel_id=1, source_target_pairs={{0,1},{1,0},{2,3},{3,2},{4,5},{5,4},{6,7},{7,6},{8,9},{9,8},{10,11... | collective-permute-start | bytes 1572872 | tf_op jit(solution)/shard_map/gather_near/ppermute | solution.py:441
  7.2 6.3 %load.1 = (bf16[384,2048]{1,0:T(8,128)(2,1)S(1)}, f32[192,1024]{1,0:T(8,128)S(1)}, bf16[256,1024]{1,0:T(8,128)(2,1)}, bf16[2048,1536]{1,0:T(8,128)(2,1)S(1)}, f32[1024,1536]{1,0:T(8,128)S(1)}) custom-call(s32[1]{0:T(128)} %bitcast.place, bf16[2048,1536]{1,0:T(8,128)(2,1)} %refs_7_.1, bf16[1,1024,1536]{2,1,0:T(8,128)(2,1)} %momentum.1, ...), custom_call_target="tpu_custom_call" | custom-call | flops 2415919104 | bytes 9437184 | tf_op jit(solution)/shard_map/gather_near/load/pallas_call | solution.py:280
  13.5 1.6 %collective-permute-done.refs_1_ = bf16[256,1024]{1,0:T(8,128)(2,1)S(1)} collective-permute-done((bf16[256,1024]{1,0:T(8,128)(2,1)}, bf16[256,1024]{1,0:T(8,128)(2,1)S(1)}, u32[]{:S(2)}, u32[]{:S(2)}) %collective-permute-start) | collective-permute-done | bytes 524320 | tf_op jit(solution)/shard_map/gather_near/ppermute | solution.py:444
  15.2 1.2 %collective-permute-start.7 = (bf16[256,1024]{1,0:T(8,128)(2,1)S(1)}, bf16[256,1024]{1,0:T(8,128)(2,1)S(1)}, u32[]{:S(2)}, u32[]{:S(2)}) collective-permute-start(bf16[256,1024]{1,0:T(8,128)(2,1)S(1)} %collective-permute-done.refs_1_), channel_id=1, source_target_pairs={{0,1},{1,0},{2,3},{3,2},{4,5},{5,4},{6,7},{7,6},{8,9},{9,8},{10,11... | collective-permute-start | bytes 1572872 | tf_op jit(solution)/shard_map/gather_middle/ppermute | solution.py:441
  17.0 2.1 %collective-permute-done.3.refs_2_ = bf16[256,1024]{1,0:T(8,128)(2,1)S(1)} collective-permute-done((bf16[256,1024]{1,0:T(8,128)(2,1)}, bf16[256,1024]{1,0:T(8,128)(2,1)S(1)}, u32[]{:S(2)}, u32[]{:S(2)}) %collective-permute-start.3) | collective-permute-done | bytes 524320 | tf_op jit(solution)/shard_map/gather_near/ppermute | solution.py:447
  19.9 0.8 collective-permute-start.5
  20.7 2.0 %collective-permute-start.9 = (bf16[128,1024]{1,0:T(8,128)(2,1)S(1)}, bf16[128,1024]{1,0:T(8,128)(2,1)S(1)}, u32[]{:S(2)}, u32[]{:S(2)}) collective-permute-start(bf16[128,1024]{1,0:T(8,128)(2,1)S(1)} %get-tuple-element.64), channel_id=1, source_target_pairs={{0,6},{2,0},{4,2},{6,4},{1,7},{3,1},{5,3},{7,5},{8,14},{10,8},{12,... | collective-permute-start | bytes 786440 | tf_op jit(solution)/shard_map/gather_middle/ppermute | solution.py:444
  22.6 3.1 %add.139.refs_5_ = f32[1024,1536]{1,0:T(8,128)} custom-call(s32[3]{0:T(128)S(1)} %get-tuple-element.42.places, bf16[256,1024]{1,0:T(8,128)(2,1)S(1)} %collective-permute-done.2.refs_0_, bf16[256,1024]{1,0:T(8,128)(2,1)S(1)} %collective-permute-done.refs_1_, bf16[256,1024]{1,0:T(8,128)(2,1)S(1)} %collective-permute-done.3.refs_2_, ...), custom_call_target="tpu_custom_call" | custom-call | flops 1207959552 | bytes 3145728 | tf_op jit(solution)/shard_map/add/pallas_call | solution.py:308
  26.1 0.8 collective-permute-done.5.refs_2_
  26.9 1.3 %tally.2.refs_6_ = f32[192,1024]{1,0:T(8,128)S(1)} custom-call(s32[3]{0:T(128)S(1)} %get-tuple-element.42.places, bf16[256,1024]{1,0:T(8,128)(2,1)S(1)} %collective-permute-done.2.refs_0_, bf16[256,1024]{1,0:T(8,128)(2,1)S(1)} %collective-permute-done.refs_1_, bf16[256,1024]{1,0:T(8,128)(2,1)S(1)} %collective-permute-done.3.refs_2_, ...), custom_call_target="tpu_custom_call" | custom-call | flops 603979776 | tf_op jit(solution)/shard_map/tally/pallas_call | solution.py:324
  28.2 3.1 %add.140.refs_8_ = f32[1024,1536]{1,0:T(8,128)} custom-call(s32[3]{0:T(128)S(1)} %get-tuple-element.42.places, bf16[256,1024]{1,0:T(8,128)(2,1)S(1)} %collective-permute-done.2.refs_0_, bf16[256,1024]{1,0:T(8,128)(2,1)S(1)} %collective-permute-done.refs_1_, bf16[256,1024]{1,0:T(8,128)(2,1)S(1)} %collective-permute-done.3.refs_2_, ...), custom_call_target="tpu_custom_call", output_to_operand_aliasing={{}: (6, {})} | custom-call | flops 1207959552 | bytes 3145728 | tf_op jit(solution)/shard_map/add/pallas_call | solution.py:308
  31.3 1.2 %collective-permute-done.8.refs_1_ = bf16[128,1024]{1,0:T(8,128)(2,1)S(1)} collective-permute-done((bf16[128,1024]{1,0:T(8,128)(2,1)S(1)}, bf16[128,1024]{1,0:T(8,128)(2,1)S(1)}, u32[]{:S(2)}, u32[]{:S(2)}) %collective-permute-start.8) | collective-permute-done | bytes 262176 | tf_op jit(solution)/shard_map/gather_middle/ppermute | solution.py:447
  32.5 1.3 %tally.3.refs_3_ = f32[192,1024]{1,0:T(8,128)S(1)} custom-call(s32[3]{0:T(128)S(1)} %get-tuple-element.49.places, bf16[256,1024]{1,0:T(8,128)(2,1)S(1)} %collective-permute-done.7.refs_0_, bf16[128,1024]{1,0:T(8,128)(2,1)S(1)} %collective-permute-done.8.refs_1_, bf16[128,1024]{1,0:T(8,128)(2,1)S(1)} %collective-permute-done.5.refs_2_, ...), custom_call_target="tpu_custom_call" | custom-call | flops 603979776 | tf_op jit(solution)/shard_map/tally/pallas_call | solution.py:324
  33.9 4.2 %collective-permute-done.6.refs_1_.refs_6_ = bf16[128,1024]{1,0:T(8,128)(2,1)S(1)} collective-permute-done((bf16[128,1024]{1,0:T(8,128)(2,1)S(1)}, bf16[128,1024]{1,0:T(8,128)(2,1)S(1)}, u32[]{:S(2)}, u32[]{:S(2)}) %collective-permute-start.6) | collective-permute-done | bytes 262176 | tf_op jit(solution)/shard_map/gather_far/ppermute | solution.py:447
  38.5 3.1 %collective-permute-start.10 = (f32[768,128]{1,0:T(8,128)S(1)}, f32[768,128]{1,0:T(8,128)S(1)}, u32[]{:S(2)}, u32[]{:S(2)}) collective-permute-start(f32[768,128]{1,0:T(8,128)S(1)} %get-tuple-element.54), channel_id=1, source_target_pairs={{0,8},{8,0},{1,9},{9,1},{2,10},{10,2},{3,11},{11,3},{4,12},{12,4},... | collective-permute-start | bytes 1179656 | tf_op jit(solution)/shard_map/sum_core/ppermute | solution.py:482
  41.6 0.9 save.1.refs_9_
  43.7 10.5 %all-to-all-start = ((f32[16,48,128]{2,1,0:T(8,128)}), f32[16,48,128]{2,1,0:T(8,128)S(1)}, u32[]{:S(2)}, u32[]{:S(2)}) async-start(f32[16,48,128]{2,1,0:T(8,128)} %bitcast.17), calls=%async_computation | async-start | bytes 786432 | tf_op jit(solution)/shard_map/sum_chips/all_to_all | solution.py:485
  54.2 9.3 %finish.1 = bf16[1,1024,1536]{2,1,0:T(8,128)(2,1)} custom-call(s32[4]{0:T(128)S(1)} %pad_add_fusion.2.places, bf16[256,1024]{1,0:T(8,128)(2,1)} %copy-done, bf16[128,1024]{1,0:T(8,128)(2,1)} %copy-done.4, bf16[128,1024]{1,0:T(8,128)(2,1)} %copy-done.2, bf16[128,1024]{1,0:T(8,128)(2,1)} %copy-done.1, bf16[128,1024]{1,0:T(8,128)(2,1)} %copy-done.3, ...), custom_call_target="tpu_custom_call" | custom-call | flops 6442450944 | bytes 9437184 | tf_op jit(solution)/shard_map/finish/pallas_call | solution.py:355
  63.6 5.6 %all-to-all-done = f32[16,48,128]{2,1,0:T(8,128)S(1)} async-done(((f32[16,48,128]{2,1,0:T(8,128)}), f32[16,48,128]{2,1,0:T(8,128)S(1)}, u32[]{:S(2)}, u32[]{:S(2)}) %all-to-all-start) | async-done | bytes 393248 | tf_op jit(solution)/shard_map/sum_chips/all_to_all | solution.py:485
  69.3 16.2 %all_to_all.23 = s16[16,64,128]{2,1,0:T(8,128)(2,1)S(1)} all-to-all(s16[16,64,128]{2,1,0:T(8,128)(2,1)S(1)} %bitcast.16), channel_id=1, replica_groups=mesh['z'=8,'xh'=2,'core'=2,'y'=4,'xl'=2] {'z','xh'}, dimensions={0} | all-to-all | bytes 524288 | tf_op jit(solution)/shard_map/spread_chips/all_to_all | solution.py:489
  85.5 2.2 %collective-permute-start.11 = (s16[1024,128]{1,0:T(8,128)(2,1)S(1)}, s16[1024,128]{1,0:T(8,128)(2,1)S(1)}, u32[]{:S(2)}, u32[]{:S(2)}) collective-permute-start(s16[1024,128]{1,0:T(8,128)(2,1)S(1)} %bitcast.14), channel_id=1, source_target_pairs={{0,8},{8,0},{1,9},{9,1},{2,10},{10,2},{3,11},{11,3},{4,12},{12,4},... | collective-permute-start | bytes 786440 | tf_op jit(solution)/shard_map/spread_core/ppermute | solution.py:491
  87.7 1.5 %update.2.refs_0_ = bf16[1024,1536]{1,0:T(8,128)(2,1)} custom-call(s32[1]{0:T(128)} %bitcast.8.core.where, s16[1024,128]{1,0:T(8,128)(2,1)S(1)} %bitcast.15, bf16[96,256]{1,0:T(8,128)(2,1)S(1)} %pad_maximum_fusion.refs_10_.stacked), custom_call_target="tpu_custom_call" | custom-call | flops 150994944 | bytes 1572864 | tf_op jit(solution)/shard_map/update/pallas_call | solution.py:413
  89.2 1.5 %update.3 = bf16[1024,1536]{1,0:T(8,128)(2,1)} custom-call(s32[1]{0:T(128)S(6)} %sub.7.where, s16[1024,128]{1,0:T(8,128)(2,1)S(1)} %collective-permute-done.11.whole, bf16[96,256]{1,0:T(8,128)(2,1)S(1)} %pad_maximum_fusion.refs_10_.stacked, bf16[1024,1536]{1,0:T(8,128)(2,1)} %update.2.refs_0_), custom_call_target="tpu_custom_call", output_to_operand_aliasing={{}: (3, {})} | custom-call | flops 150994944 | bytes 1572864 | tf_op jit(solution)/shard_map/update/pallas_call | solution.py:413
  (39 shorter events, 5.1 us)
Async XLA Ops:
  0.6 14.5 %collective-permute-start = (bf16[256,1024]{1,0:T(8,128)(2,1)}, bf16[256,1024]{1,0:T(8,128)(2,1)S(1)}, u32[]{:S(2)}, u32[]{:S(2)}) collective-permute-start(bf16[256,1024]{1,0:T(8,128)(2,1)} %x_rows.1), channel_id=1, source_target_pairs={{0,6},{2,0},{4,2},{6,4},{1,7},{3,1},{5,3},{7,5},{8,14},{10,8},{12,... | collective-permute-start | bytes 1572872 | tf_op jit(solution)/shard_map/gather_near/ppermute | solution.py:444
  4.3 12.7 %collective-permute-start.2 = (bf16[256,1024]{1,0:T(8,128)(2,1)}, bf16[256,1024]{1,0:T(8,128)(2,1)S(1)}, u32[]{:S(2)}, u32[]{:S(2)}) collective-permute-start(bf16[256,1024]{1,0:T(8,128)(2,1)} %x_rows.1), channel_id=1, source_target_pairs={{0,1},{1,0},{2,3},{3,2},{4,5},{5,4},{6,7},{7,6},{8,9},{9,8},{10,11... | collective-permute-start | bytes 1572872 | tf_op jit(solution)/shard_map/gather_near/ppermute | solution.py:441
  5.5 13.6 %collective-permute-start.3 = (bf16[256,1024]{1,0:T(8,128)(2,1)}, bf16[256,1024]{1,0:T(8,128)(2,1)S(1)}, u32[]{:S(2)}, u32[]{:S(2)}) collective-permute-start(bf16[256,1024]{1,0:T(8,128)(2,1)} %x_rows.1), channel_id=1, source_target_pairs={{0,2},{2,4},{4,6},{6,0},{1,3},{3,5},{5,7},{7,1},{8,10},{10,12},{12... | collective-permute-start | bytes 1572872 | tf_op jit(solution)/shard_map/gather_near/ppermute | solution.py:447
  15.2 17.3 %collective-permute-start.7 = (bf16[256,1024]{1,0:T(8,128)(2,1)S(1)}, bf16[256,1024]{1,0:T(8,128)(2,1)S(1)}, u32[]{:S(2)}, u32[]{:S(2)}) collective-permute-start(bf16[256,1024]{1,0:T(8,128)(2,1)S(1)} %collective-permute-done.refs_1_), channel_id=1, source_target_pairs={{0,1},{1,0},{2,3},{3,2},{4,5},{5,4},{6,7},{7,6},{8,9},{9,8},{10,11... | collective-permute-start | bytes 1572872 | tf_op jit(solution)/shard_map/gather_middle/ppermute | solution.py:441
  19.1 6.6 %collective-permute-start.1 = (bf16[128,1024]{1,0:T(8,128)(2,1)S(1)}, bf16[128,1024]{1,0:T(8,128)(2,1)S(1)}, u32[]{:S(2)}, u32[]{:S(2)}) collective-permute-start(bf16[128,1024]{1,0:T(8,128)(2,1)S(1)} %get-tuple-element.65), channel_id=1, source_target_pairs={{0,6},{2,0},{4,2},{6,4},{1,7},{3,1},{5,3},{7,5},{8,14},{10,8},{12,... | collective-permute-start | bytes 786440 | tf_op jit(solution)/shard_map/gather_middle/ppermute | solution.py:444
  19.9 7.0 %collective-permute-start.5 = (bf16[128,1024]{1,0:T(8,128)(2,1)S(1)}, bf16[128,1024]{1,0:T(8,128)(2,1)S(1)}, u32[]{:S(2)}, u32[]{:S(2)}) collective-permute-start(bf16[128,1024]{1,0:T(8,128)(2,1)S(1)} %get-tuple-element.67), channel_id=1, source_target_pairs={{0,2},{2,4},{4,6},{6,0},{1,3},{3,5},{5,7},{7,1},{8,10},{10,12},{12... | collective-permute-start | bytes 786440 | tf_op jit(solution)/shard_map/gather_middle/ppermute | solution.py:447
  20.7 10.6 %collective-permute-start.9 = (bf16[128,1024]{1,0:T(8,128)(2,1)S(1)}, bf16[128,1024]{1,0:T(8,128)(2,1)S(1)}, u32[]{:S(2)}, u32[]{:S(2)}) collective-permute-start(bf16[128,1024]{1,0:T(8,128)(2,1)S(1)} %get-tuple-element.64), channel_id=1, source_target_pairs={{0,6},{2,0},{4,2},{6,4},{1,7},{3,1},{5,3},{7,5},{8,14},{10,8},{12,... | collective-permute-start | bytes 786440 | tf_op jit(solution)/shard_map/gather_middle/ppermute | solution.py:444
  22.6 9.8 %collective-permute-start.8 = (bf16[128,1024]{1,0:T(8,128)(2,1)S(1)}, bf16[128,1024]{1,0:T(8,128)(2,1)S(1)}, u32[]{:S(2)}, u32[]{:S(2)}) collective-permute-start(bf16[128,1024]{1,0:T(8,128)(2,1)S(1)} %get-tuple-element.66), channel_id=1, source_target_pairs={{0,2},{2,4},{4,6},{6,0},{1,3},{3,5},{5,7},{7,1},{8,10},{10,12},{12... | collective-permute-start | bytes 786440 | tf_op jit(solution)/shard_map/gather_middle/ppermute | solution.py:447
  25.7 6.8 %copy-start.1 = (bf16[128,1024]{1,0:T(8,128)(2,1)}, bf16[128,1024]{1,0:T(8,128)(2,1)S(1)}, u32[]{:S(2)}) copy-start(bf16[128,1024]{1,0:T(8,128)(2,1)S(1)} %collective-permute-done.1.refs_3_) | copy-start | bytes 786436
  25.7 8.1 %collective-permute-start.4 = (bf16[128,1024]{1,0:T(8,128)(2,1)S(1)}, bf16[128,1024]{1,0:T(8,128)(2,1)S(1)}, u32[]{:S(2)}, u32[]{:S(2)}) collective-permute-start(bf16[128,1024]{1,0:T(8,128)(2,1)S(1)} %collective-permute-done.1.refs_3_), channel_id=1, source_target_pairs={{0,1},{1,0},{2,3},{3,2},{4,5},{5,4},{6,7},{7,6},{8,9},{9,8},{10,11... | collective-permute-start | bytes 786440 | tf_op jit(solution)/shard_map/gather_far/ppermute | solution.py:441
  26.9 5.6 %copy-start.2 = (bf16[128,1024]{1,0:T(8,128)(2,1)}, bf16[128,1024]{1,0:T(8,128)(2,1)S(1)}, u32[]{:S(2)}) copy-start(bf16[128,1024]{1,0:T(8,128)(2,1)S(1)} %collective-permute-done.5.refs_2_) | copy-start | bytes 786436
  26.9 11.2 %collective-permute-start.6 = (bf16[128,1024]{1,0:T(8,128)(2,1)S(1)}, bf16[128,1024]{1,0:T(8,128)(2,1)S(1)}, u32[]{:S(2)}, u32[]{:S(2)}) collective-permute-start(bf16[128,1024]{1,0:T(8,128)(2,1)S(1)} %collective-permute-done.5.refs_2_), channel_id=1, source_target_pairs={{0,2},{2,4},{4,6},{6,0},{1,3},{3,5},{5,7},{7,1},{8,10},{10,12},{12... | collective-permute-start | bytes 786440 | tf_op jit(solution)/shard_map/gather_far/ppermute | solution.py:447
  31.3 22.9 %copy-start.3 = (bf16[128,1024]{1,0:T(8,128)(2,1)}, bf16[128,1024]{1,0:T(8,128)(2,1)S(1)}, u32[]{:S(2)}) copy-start(bf16[128,1024]{1,0:T(8,128)(2,1)S(1)} %collective-permute-done.9.refs_4_) | copy-start | bytes 786436
  32.5 21.7 %copy-start.4 = (bf16[128,1024]{1,0:T(8,128)(2,1)}, bf16[128,1024]{1,0:T(8,128)(2,1)S(1)}, u32[]{:S(2)}) copy-start(bf16[128,1024]{1,0:T(8,128)(2,1)S(1)} %collective-permute-done.8.refs_1_) | copy-start | bytes 786436
  32.5 21.7 %copy-start = (bf16[256,1024]{1,0:T(8,128)(2,1)}, bf16[256,1024]{1,0:T(8,128)(2,1)S(1)}, u32[]{:S(2)}) copy-start(bf16[256,1024]{1,0:T(8,128)(2,1)S(1)} %collective-permute-done.7.refs_0_) | copy-start | bytes 1572868
  33.8 20.4 %copy-start.5 = (bf16[128,1024]{1,0:T(8,128)(2,1)}, bf16[128,1024]{1,0:T(8,128)(2,1)S(1)}, u32[]{:S(2)}) copy-start(bf16[128,1024]{1,0:T(8,128)(2,1)S(1)} %collective-permute-done.4.refs_0_.refs_5_) | copy-start | bytes 786436
  38.1 5.6 %copy-start.6 = (bf16[128,1024]{1,0:T(8,128)(2,1)}, bf16[128,1024]{1,0:T(8,128)(2,1)S(1)}, u32[]{:S(2)}) copy-start(bf16[128,1024]{1,0:T(8,128)(2,1)S(1)} %collective-permute-done.6.refs_1_.refs_6_) | copy-start | bytes 786436
  38.5 4.5 %collective-permute-start.10 = (f32[768,128]{1,0:T(8,128)S(1)}, f32[768,128]{1,0:T(8,128)S(1)}, u32[]{:S(2)}, u32[]{:S(2)}) collective-permute-start(f32[768,128]{1,0:T(8,128)S(1)} %get-tuple-element.54), channel_id=1, source_target_pairs={{0,8},{8,0},{1,9},{9,1},{2,10},{10,2},{3,11},{11,3},{4,12},{12,4},... | collective-permute-start | bytes 1179656 | tf_op jit(solution)/shard_map/sum_core/ppermute | solution.py:482
  43.7 25.5 %all-to-all-start = ((f32[16,48,128]{2,1,0:T(8,128)}), f32[16,48,128]{2,1,0:T(8,128)S(1)}, u32[]{:S(2)}, u32[]{:S(2)}) async-start(f32[16,48,128]{2,1,0:T(8,128)} %bitcast.17), calls=%async_computation | async-start | bytes 786432 | tf_op jit(solution)/shard_map/sum_chips/all_to_all | solution.py:485
  85.5 3.7 %collective-permute-start.11 = (s16[1024,128]{1,0:T(8,128)(2,1)S(1)}, s16[1024,128]{1,0:T(8,128)(2,1)S(1)}, u32[]{:S(2)}, u32[]{:S(2)}) collective-permute-start(s16[1024,128]{1,0:T(8,128)(2,1)S(1)} %bitcast.14), channel_id=1, source_target_pairs={{0,8},{8,0},{1,9},{9,1},{2,10},{10,2},{3,11},{11,3},{4,12},{12,4},... | collective-permute-start | bytes 786440 | tf_op jit(solution)/shard_map/spread_core/ppermute | solution.py:491

commit v5 on v4

--- a/solution.py
+++ b/solution.py
@@ -240,12 +240,11 @@
     kept = value.shape[0] // tiles
     span = pl.ds(pl.multiple_of(where[0] * staged.shape[0], staged.shape[0]), staged.shape[0])
     outs = []
-    for w in range(staged.shape[1] // TILE):
-        for b in range(w * TILE // GROUP, (w + 1) * TILE // GROUP):
-            parts = [value[t * kept + b * band : t * kept + (b + 1) * band] for t in range(tiles)]
-            staged[:, block(b, GROUP)] = decode(jnp.concatenate(parts, axis=1), stacked[...]).astype(BF16)
-        wide = block(w, TILE)
-        outs.append(pltpu.make_async_copy(staged.at[:, wide], update.at[span, wide], sems.at[w]))
+    for b in range(staged.shape[1] // GROUP):
+        parts = [value[t * kept + b * band : t * kept + (b + 1) * band] for t in range(tiles)]
+        wide = block(b, GROUP)
+        staged[:, wide] = decode(jnp.concatenate(parts, axis=1), stacked[...]).astype(BF16)
+        outs.append(pltpu.make_async_copy(staged.at[:, wide], update.at[span, wide], sems.at[b]))
         outs[-1].start()
     for out in outs:
         out.wait()
@@ -416,7 +415,7 @@
         out_specs=ANY,
         out_shape=jax.ShapeDtypeStruct((rows, columns), BF16),
         input_output_aliases={3: 0} if others else {},
-        scratch_shapes=[pltpu.VMEM((rows // 2, columns), BF16), pltpu.SemaphoreType.DMA((columns // TILE,))],
+        scratch_shapes=[pltpu.VMEM((rows // 2, columns), BF16), pltpu.SemaphoreType.DMA((columns // GROUP,))],
         compiler_params=params(16),
         cost_estimate=estimate(rows * columns * 96, rows * columns),
         name="update",

time: 91.1 us -> 91.1 us (level)
  no operation moved by 1% of the time
where the time goes in v5:
time: 91.1 us; the launch traced here: 90.9 us
  Pallas kernels  29.6 us (32%)
  starting transfers between devices  25.7 us (28%)
  waiting for transfers between devices  16.6 us (18%)
  blocking collectives  16.2 us (18%)
  other arithmetic  1.68 us (2%)
  between operations  1.03 us (1%)
    all_to_all x1, blocking collectives, shards(): whole = lax.all_to_all(sum_parts(parts, 16), ('z', 'xh'), 0, 0, tiled=True)  16.2 us
    all_to_all x1, starting transfers between devices, shards(): parts = lax.all_to_all(mine, ('z', 'xh'), 0, 0, tiled=True)  10.5 us
    pallas_call x1, Pallas kernels, finish(): pl.pallas_call(functools.partial(fresh_kernel, groups, band), in_specs=[S...  9.34 us
    ppermute x4, waiting for transfers between devices, from_below(): return lax.ppermute(v, 'y', ring(4, 1))  8.33 us
    ppermute x3, starting transfers between devices, from_above(): return lax.ppermute(v, 'y', ring(4, -1))  6.35 us
    pallas_call x1, Pallas kernels, load(): pl.pallas_call(functools.partial(load_kernel, band), in_specs=[SMEM, ANY,...  6.34 us
    pallas_call x2, Pallas kernels, add(): pl.pallas_call(functools.partial(add_kernel, groups, span), in_specs=[SME...  6.13 us
    all_to_all x1, waiting for transfers between devices, shards(): parts = lax.all_to_all(mine, ('z', 'xh'), 0, 0, tiled=True)  5.6 us
  transfers between devices with their start and end apart: 13, of which 8 were waited for; matrix products, arithmetic and copies ran while one was open for 2% of the time, Pallas kernels for 30%

profile of v5, /device:TPU:1, one launch (start us, length us, event | category | flops | bytes accessed | tf_op | source)
XLA Modules:
  0.0 90.9 jit_solution(13194992174981716718)
XLA Ops:
  0.6 3.6 %collective-permute-start = (bf16[256,1024]{1,0:T(8,128)(2,1)}, bf16[256,1024]{1,0:T(8,128)(2,1)S(1)}, u32[]{:S(2)}, u32[]{:S(2)}) collective-permute-start(bf16[256,1024]{1,0:T(8,128)(2,1)} %x_rows.1), channel_id=1, source_target_pairs={{0,6},{2,0},{4,2},{6,4},{1,7},{3,1},{5,3},{7,5},{8,14},{10,8},{12,... | collective-permute-start | bytes 1572872 | tf_op jit(solution)/shard_map/gather_near/ppermute | solution.py:443
  4.3 1.2 %collective-permute-start.2 = (bf16[256,1024]{1,0:T(8,128)(2,1)}, bf16[256,1024]{1,0:T(8,128)(2,1)S(1)}, u32[]{:S(2)}, u32[]{:S(2)}) collective-permute-start(bf16[256,1024]{1,0:T(8,128)(2,1)} %x_rows.1), channel_id=1, source_target_pairs={{0,1},{1,0},{2,3},{3,2},{4,5},{5,4},{6,7},{7,6},{8,9},{9,8},{10,11... | collective-permute-start | bytes 1572872 | tf_op jit(solution)/shard_map/gather_near/ppermute | solution.py:440
  7.2 6.3 %load.1 = (bf16[384,2048]{1,0:T(8,128)(2,1)S(1)}, f32[192,1024]{1,0:T(8,128)S(1)}, bf16[256,1024]{1,0:T(8,128)(2,1)}, bf16[2048,1536]{1,0:T(8,128)(2,1)S(1)}, f32[1024,1536]{1,0:T(8,128)S(1)}) custom-call(s32[1]{0:T(128)} %bitcast.place, bf16[2048,1536]{1,0:T(8,128)(2,1)} %refs_7_.1, bf16[1,1024,1536]{2,1,0:T(8,128)(2,1)} %momentum.1, ...), custom_call_target="tpu_custom_call" | custom-call | flops 2415919104 | bytes 9437184 | tf_op jit(solution)/shard_map/gather_near/load/pallas_call | solution.py:279
  13.5 1.6 %collective-permute-done.refs_1_ = bf16[256,1024]{1,0:T(8,128)(2,1)S(1)} collective-permute-done((bf16[256,1024]{1,0:T(8,128)(2,1)}, bf16[256,1024]{1,0:T(8,128)(2,1)S(1)}, u32[]{:S(2)}, u32[]{:S(2)}) %collective-permute-start) | collective-permute-done | bytes 524320 | tf_op jit(solution)/shard_map/gather_near/ppermute | solution.py:443
  15.2 1.2 %collective-permute-start.7 = (bf16[256,1024]{1,0:T(8,128)(2,1)S(1)}, bf16[256,1024]{1,0:T(8,128)(2,1)S(1)}, u32[]{:S(2)}, u32[]{:S(2)}) collective-permute-start(bf16[256,1024]{1,0:T(8,128)(2,1)S(1)} %collective-permute-done.refs_1_), channel_id=1, source_target_pairs={{0,1},{1,0},{2,3},{3,2},{4,5},{5,4},{6,7},{7,6},{8,9},{9,8},{10,11... | collective-permute-start | bytes 1572872 | tf_op jit(solution)/shard_map/gather_middle/ppermute | solution.py:440
  17.0 2.1 %collective-permute-done.3.refs_2_ = bf16[256,1024]{1,0:T(8,128)(2,1)S(1)} collective-permute-done((bf16[256,1024]{1,0:T(8,128)(2,1)}, bf16[256,1024]{1,0:T(8,128)(2,1)S(1)}, u32[]{:S(2)}, u32[]{:S(2)}) %collective-permute-start.3) | collective-permute-done | bytes 524320 | tf_op jit(solution)/shard_map/gather_near/ppermute | solution.py:446
  19.9 0.8 collective-permute-start.5
  20.7 2.0 %collective-permute-start.9 = (bf16[128,1024]{1,0:T(8,128)(2,1)S(1)}, bf16[128,1024]{1,0:T(8,128)(2,1)S(1)}, u32[]{:S(2)}, u32[]{:S(2)}) collective-permute-start(bf16[128,1024]{1,0:T(8,128)(2,1)S(1)} %get-tuple-element.64), channel_id=1, source_target_pairs={{0,6},{2,0},{4,2},{6,4},{1,7},{3,1},{5,3},{7,5},{8,14},{10,8},{12,... | collective-permute-start | bytes 786440 | tf_op jit(solution)/shard_map/gather_middle/ppermute | solution.py:443
  22.6 3.1 %add.139.refs_5_ = f32[1024,1536]{1,0:T(8,128)} custom-call(s32[3]{0:T(128)S(1)} %get-tuple-element.42.places, bf16[256,1024]{1,0:T(8,128)(2,1)S(1)} %collective-permute-done.2.refs_0_, bf16[256,1024]{1,0:T(8,128)(2,1)S(1)} %collective-permute-done.refs_1_, bf16[256,1024]{1,0:T(8,128)(2,1)S(1)} %collective-permute-done.3.refs_2_, ...), custom_call_target="tpu_custom_call" | custom-call | flops 1207959552 | bytes 3145728 | tf_op jit(solution)/shard_map/add/pallas_call | solution.py:307
  26.1 0.8 collective-permute-done.5.refs_2_
  26.9 1.3 %tally.2.refs_6_ = f32[192,1024]{1,0:T(8,128)S(1)} custom-call(s32[3]{0:T(128)S(1)} %get-tuple-element.42.places, bf16[256,1024]{1,0:T(8,128)(2,1)S(1)} %collective-permute-done.2.refs_0_, bf16[256,1024]{1,0:T(8,128)(2,1)S(1)} %collective-permute-done.refs_1_, bf16[256,1024]{1,0:T(8,128)(2,1)S(1)} %collective-permute-done.3.refs_2_, ...), custom_call_target="tpu_custom_call" | custom-call | flops 603979776 | tf_op jit(solution)/shard_map/tally/pallas_call | solution.py:323
  28.2 3.1 %add.140.refs_8_ = f32[1024,1536]{1,0:T(8,128)} custom-call(s32[3]{0:T(128)S(1)} %get-tuple-element.42.places, bf16[256,1024]{1,0:T(8,128)(2,1)S(1)} %collective-permute-done.2.refs_0_, bf16[256,1024]{1,0:T(8,128)(2,1)S(1)} %collective-permute-done.refs_1_, bf16[256,1024]{1,0:T(8,128)(2,1)S(1)} %collective-permute-done.3.refs_2_, ...), custom_call_target="tpu_custom_call", output_to_operand_aliasing={{}: (6, {})} | custom-call | flops 1207959552 | bytes 3145728 | tf_op jit(solution)/shard_map/add/pallas_call | solution.py:307
  31.3 1.2 %collective-permute-done.8.refs_1_ = bf16[128,1024]{1,0:T(8,128)(2,1)S(1)} collective-permute-done((bf16[128,1024]{1,0:T(8,128)(2,1)S(1)}, bf16[128,1024]{1,0:T(8,128)(2,1)S(1)}, u32[]{:S(2)}, u32[]{:S(2)}) %collective-permute-start.8) | collective-permute-done | bytes 262176 | tf_op jit(solution)/shard_map/gather_middle/ppermute | solution.py:446
  32.5 1.3 %tally.3.refs_3_ = f32[192,1024]{1,0:T(8,128)S(1)} custom-call(s32[3]{0:T(128)S(1)} %get-tuple-element.49.places, bf16[256,1024]{1,0:T(8,128)(2,1)S(1)} %collective-permute-done.7.refs_0_, bf16[128,1024]{1,0:T(8,128)(2,1)S(1)} %collective-permute-done.8.refs_1_, bf16[128,1024]{1,0:T(8,128)(2,1)S(1)} %collective-permute-done.5.refs_2_, ...), custom_call_target="tpu_custom_call" | custom-call | flops 603979776 | tf_op jit(solution)/shard_map/tally/pallas_call | solution.py:323
  33.9 4.2 %collective-permute-done.6.refs_1_.refs_6_ = bf16[128,1024]{1,0:T(8,128)(2,1)S(1)} collective-permute-done((bf16[128,1024]{1,0:T(8,128)(2,1)S(1)}, bf16[128,1024]{1,0:T(8,128)(2,1)S(1)}, u32[]{:S(2)}, u32[]{:S(2)}) %collective-permute-start.6) | collective-permute-done | bytes 262176 | tf_op jit(solution)/shard_map/gather_far/ppermute | solution.py:446
  38.5 3.1 %collective-permute-start.10 = (f32[768,128]{1,0:T(8,128)S(1)}, f32[768,128]{1,0:T(8,128)S(1)}, u32[]{:S(2)}, u32[]{:S(2)}) collective-permute-start(f32[768,128]{1,0:T(8,128)S(1)} %get-tuple-element.54), channel_id=1, source_target_pairs={{0,8},{8,0},{1,9},{9,1},{2,10},{10,2},{3,11},{11,3},{4,12},{12,4},... | collective-permute-start | bytes 1179656 | tf_op jit(solution)/shard_map/sum_core/ppermute | solution.py:481
  41.6 0.9 save.1.refs_9_
  43.7 10.5 %all-to-all-start = ((f32[16,48,128]{2,1,0:T(8,128)}), f32[16,48,128]{2,1,0:T(8,128)S(1)}, u32[]{:S(2)}, u32[]{:S(2)}) async-start(f32[16,48,128]{2,1,0:T(8,128)} %bitcast.17), calls=%async_computation | async-start | bytes 786432 | tf_op jit(solution)/shard_map/sum_chips/all_to_all | solution.py:484
  54.2 9.3 %finish.1 = bf16[1,1024,1536]{2,1,0:T(8,128)(2,1)} custom-call(s32[4]{0:T(128)S(1)} %pad_add_fusion.2.places, bf16[256,1024]{1,0:T(8,128)(2,1)} %copy-done, bf16[128,1024]{1,0:T(8,128)(2,1)} %copy-done.4, bf16[128,1024]{1,0:T(8,128)(2,1)} %copy-done.2, bf16[128,1024]{1,0:T(8,128)(2,1)} %copy-done.1, bf16[128,1024]{1,0:T(8,128)(2,1)} %copy-done.3, ...), custom_call_target="tpu_custom_call" | custom-call | flops 6442450944 | bytes 9437184 | tf_op jit(solution)/shard_map/finish/pallas_call | solution.py:354
  63.6 5.6 %all-to-all-done = f32[16,48,128]{2,1,0:T(8,128)S(1)} async-done(((f32[16,48,128]{2,1,0:T(8,128)}), f32[16,48,128]{2,1,0:T(8,128)S(1)}, u32[]{:S(2)}, u32[]{:S(2)}) %all-to-all-start) | async-done | bytes 393248 | tf_op jit(solution)/shard_map/sum_chips/all_to_all | solution.py:484
  69.3 16.2 %all_to_all.23 = s16[16,64,128]{2,1,0:T(8,128)(2,1)S(1)} all-to-all(s16[16,64,128]{2,1,0:T(8,128)(2,1)S(1)} %bitcast.16), channel_id=1, replica_groups=mesh['z'=8,'xh'=2,'core'=2,'y'=4,'xl'=2] {'z','xh'}, dimensions={0} | all-to-all | bytes 524288 | tf_op jit(solution)/shard_map/spread_chips/all_to_all | solution.py:488
  85.5 2.2 %collective-permute-start.11 = (s16[1024,128]{1,0:T(8,128)(2,1)S(1)}, s16[1024,128]{1,0:T(8,128)(2,1)S(1)}, u32[]{:S(2)}, u32[]{:S(2)}) collective-permute-start(s16[1024,128]{1,0:T(8,128)(2,1)S(1)} %bitcast.14), channel_id=1, source_target_pairs={{0,8},{8,0},{1,9},{9,1},{2,10},{10,2},{3,11},{11,3},{4,12},{12,4},... | collective-permute-start | bytes 786440 | tf_op jit(solution)/shard_map/spread_core/ppermute | solution.py:490
  87.7 1.5 %update.2.refs_0_ = bf16[1024,1536]{1,0:T(8,128)(2,1)} custom-call(s32[1]{0:T(128)} %bitcast.8.core.where, s16[1024,128]{1,0:T(8,128)(2,1)S(1)} %bitcast.15, bf16[96,256]{1,0:T(8,128)(2,1)S(1)} %pad_maximum_fusion.refs_10_.stacked), custom_call_target="tpu_custom_call" | custom-call | flops 150994944 | bytes 1572864 | tf_op jit(solution)/shard_map/update/pallas_call | solution.py:412
  89.2 1.5 %update.3 = bf16[1024,1536]{1,0:T(8,128)(2,1)} custom-call(s32[1]{0:T(128)S(6)} %sub.7.where, s16[1024,128]{1,0:T(8,128)(2,1)S(1)} %collective-permute-done.11.whole, bf16[96,256]{1,0:T(8,128)(2,1)S(1)} %pad_maximum_fusion.refs_10_.stacked, bf16[1024,1536]{1,0:T(8,128)(2,1)} %update.2.refs_0_), custom_call_target="tpu_custom_call", output_to_operand_aliasing={{}: (3, {})} | custom-call | flops 150994944 | bytes 1572864 | tf_op jit(solution)/shard_map/update/pallas_call | solution.py:412
  (39 shorter events, 5.1 us)
Async XLA Ops:
  0.6 14.5 %collective-permute-start = (bf16[256,1024]{1,0:T(8,128)(2,1)}, bf16[256,1024]{1,0:T(8,128)(2,1)S(1)}, u32[]{:S(2)}, u32[]{:S(2)}) collective-permute-start(bf16[256,1024]{1,0:T(8,128)(2,1)} %x_rows.1), channel_id=1, source_target_pairs={{0,6},{2,0},{4,2},{6,4},{1,7},{3,1},{5,3},{7,5},{8,14},{10,8},{12,... | collective-permute-start | bytes 1572872 | tf_op jit(solution)/shard_map/gather_near/ppermute | solution.py:443
  4.3 12.7 %collective-permute-start.2 = (bf16[256,1024]{1,0:T(8,128)(2,1)}, bf16[256,1024]{1,0:T(8,128)(2,1)S(1)}, u32[]{:S(2)}, u32[]{:S(2)}) collective-permute-start(bf16[256,1024]{1,0:T(8,128)(2,1)} %x_rows.1), channel_id=1, source_target_pairs={{0,1},{1,0},{2,3},{3,2},{4,5},{5,4},{6,7},{7,6},{8,9},{9,8},{10,11... | collective-permute-start | bytes 1572872 | tf_op jit(solution)/shard_map/gather_near/ppermute | solution.py:440
  5.5 13.6 %collective-permute-start.3 = (bf16[256,1024]{1,0:T(8,128)(2,1)}, bf16[256,1024]{1,0:T(8,128)(2,1)S(1)}, u32[]{:S(2)}, u32[]{:S(2)}) collective-permute-start(bf16[256,1024]{1,0:T(8,128)(2,1)} %x_rows.1), channel_id=1, source_target_pairs={{0,2},{2,4},{4,6},{6,0},{1,3},{3,5},{5,7},{7,1},{8,10},{10,12},{12... | collective-permute-start | bytes 1572872 | tf_op jit(solution)/shard_map/gather_near/ppermute | solution.py:446
  15.2 17.3 %collective-permute-start.7 = (bf16[256,1024]{1,0:T(8,128)(2,1)S(1)}, bf16[256,1024]{1,0:T(8,128)(2,1)S(1)}, u32[]{:S(2)}, u32[]{:S(2)}) collective-permute-start(bf16[256,1024]{1,0:T(8,128)(2,1)S(1)} %collective-permute-done.refs_1_), channel_id=1, source_target_pairs={{0,1},{1,0},{2,3},{3,2},{4,5},{5,4},{6,7},{7,6},{8,9},{9,8},{10,11... | collective-permute-start | bytes 1572872 | tf_op jit(solution)/shard_map/gather_middle/ppermute | solution.py:440
  19.1 6.6 %collective-permute-start.1 = (bf16[128,1024]{1,0:T(8,128)(2,1)S(1)}, bf16[128,1024]{1,0:T(8,128)(2,1)S(1)}, u32[]{:S(2)}, u32[]{:S(2)}) collective-permute-start(bf16[128,1024]{1,0:T(8,128)(2,1)S(1)} %get-tuple-element.65), channel_id=1, source_target_pairs={{0,6},{2,0},{4,2},{6,4},{1,7},{3,1},{5,3},{7,5},{8,14},{10,8},{12,... | collective-permute-start | bytes 786440 | tf_op jit(solution)/shard_map/gather_middle/ppermute | solution.py:443
  19.9 7.0 %collective-permute-start.5 = (bf16[128,1024]{1,0:T(8,128)(2,1)S(1)}, bf16[128,1024]{1,0:T(8,128)(2,1)S(1)}, u32[]{:S(2)}, u32[]{:S(2)}) collective-permute-start(bf16[128,1024]{1,0:T(8,128)(2,1)S(1)} %get-tuple-element.67), channel_id=1, source_target_pairs={{0,2},{2,4},{4,6},{6,0},{1,3},{3,5},{5,7},{7,1},{8,10},{10,12},{12... | collective-permute-start | bytes 786440 | tf_op jit(solution)/shard_map/gather_middle/ppermute | solution.py:446
  20.7 10.6 %collective-permute-start.9 = (bf16[128,1024]{1,0:T(8,128)(2,1)S(1)}, bf16[128,1024]{1,0:T(8,128)(2,1)S(1)}, u32[]{:S(2)}, u32[]{:S(2)}) collective-permute-start(bf16[128,1024]{1,0:T(8,128)(2,1)S(1)} %get-tuple-element.64), channel_id=1, source_target_pairs={{0,6},{2,0},{4,2},{6,4},{1,7},{3,1},{5,3},{7,5},{8,14},{10,8},{12,... | collective-permute-start | bytes 786440 | tf_op jit(solution)/shard_map/gather_middle/ppermute | solution.py:443
  22.6 9.8 %collective-permute-start.8 = (bf16[128,1024]{1,0:T(8,128)(2,1)S(1)}, bf16[128,1024]{1,0:T(8,128)(2,1)S(1)}, u32[]{:S(2)}, u32[]{:S(2)}) collective-permute-start(bf16[128,1024]{1,0:T(8,128)(2,1)S(1)} %get-tuple-element.66), channel_id=1, source_target_pairs={{0,2},{2,4},{4,6},{6,0},{1,3},{3,5},{5,7},{7,1},{8,10},{10,12},{12... | collective-permute-start | bytes 786440 | tf_op jit(solution)/shard_map/gather_middle/ppermute | solution.py:446
  25.7 6.8 %copy-start.1 = (bf16[128,1024]{1,0:T(8,128)(2,1)}, bf16[128,1024]{1,0:T(8,128)(2,1)S(1)}, u32[]{:S(2)}) copy-start(bf16[128,1024]{1,0:T(8,128)(2,1)S(1)} %collective-permute-done.1.refs_3_) | copy-start | bytes 786436
  25.7 8.1 %collective-permute-start.4 = (bf16[128,1024]{1,0:T(8,128)(2,1)S(1)}, bf16[128,1024]{1,0:T(8,128)(2,1)S(1)}, u32[]{:S(2)}, u32[]{:S(2)}) collective-permute-start(bf16[128,1024]{1,0:T(8,128)(2,1)S(1)} %collective-permute-done.1.refs_3_), channel_id=1, source_target_pairs={{0,1},{1,0},{2,3},{3,2},{4,5},{5,4},{6,7},{7,6},{8,9},{9,8},{10,11... | collective-permute-start | bytes 786440 | tf_op jit(solution)/shard_map/gather_far/ppermute | solution.py:440
  26.9 5.6 %copy-start.2 = (bf16[128,1024]{1,0:T(8,128)(2,1)}, bf16[128,1024]{1,0:T(8,128)(2,1)S(1)}, u32[]{:S(2)}) copy-start(bf16[128,1024]{1,0:T(8,128)(2,1)S(1)} %collective-permute-done.5.refs_2_) | copy-start | bytes 786436
  26.9 11.2 %collective-permute-start.6 = (bf16[128,1024]{1,0:T(8,128)(2,1)S(1)}, bf16[128,1024]{1,0:T(8,128)(2,1)S(1)}, u32[]{:S(2)}, u32[]{:S(2)}) collective-permute-start(bf16[128,1024]{1,0:T(8,128)(2,1)S(1)} %collective-permute-done.5.refs_2_), channel_id=1, source_target_pairs={{0,2},{2,4},{4,6},{6,0},{1,3},{3,5},{5,7},{7,1},{8,10},{10,12},{12... | collective-permute-start | bytes 786440 | tf_op jit(solution)/shard_map/gather_far/ppermute | solution.py:446
  31.3 22.9 %copy-start.3 = (bf16[128,1024]{1,0:T(8,128)(2,1)}, bf16[128,1024]{1,0:T(8,128)(2,1)S(1)}, u32[]{:S(2)}) copy-start(bf16[128,1024]{1,0:T(8,128)(2,1)S(1)} %collective-permute-done.9.refs_4_) | copy-start | bytes 786436
  32.5 21.7 %copy-start.4 = (bf16[128,1024]{1,0:T(8,128)(2,1)}, bf16[128,1024]{1,0:T(8,128)(2,1)S(1)}, u32[]{:S(2)}) copy-start(bf16[128,1024]{1,0:T(8,128)(2,1)S(1)} %collective-permute-done.8.refs_1_) | copy-start | bytes 786436
  32.5 21.7 %copy-start = (bf16[256,1024]{1,0:T(8,128)(2,1)}, bf16[256,1024]{1,0:T(8,128)(2,1)S(1)}, u32[]{:S(2)}) copy-start(bf16[256,1024]{1,0:T(8,128)(2,1)S(1)} %collective-permute-done.7.refs_0_) | copy-start | bytes 1572868
  33.8 20.4 %copy-start.5 = (bf16[128,1024]{1,0:T(8,128)(2,1)}, bf16[128,1024]{1,0:T(8,128)(2,1)S(1)}, u32[]{:S(2)}) copy-start(bf16[128,1024]{1,0:T(8,128)(2,1)S(1)} %collective-permute-done.4.refs_0_.refs_5_) | copy-start | bytes 786436
  38.1 5.6 %copy-start.6 = (bf16[128,1024]{1,0:T(8,128)(2,1)}, bf16[128,1024]{1,0:T(8,128)(2,1)S(1)}, u32[]{:S(2)}) copy-start(bf16[128,1024]{1,0:T(8,128)(2,1)S(1)} %collective-permute-done.6.refs_1_.refs_6_) | copy-start | bytes 786436
  38.5 4.5 %collective-permute-start.10 = (f32[768,128]{1,0:T(8,128)S(1)}, f32[768,128]{1,0:T(8,128)S(1)}, u32[]{:S(2)}, u32[]{:S(2)}) collective-permute-start(f32[768,128]{1,0:T(8,128)S(1)} %get-tuple-element.54), channel_id=1, source_target_pairs={{0,8},{8,0},{1,9},{9,1},{2,10},{10,2},{3,11},{11,3},{4,12},{12,4},... | collective-permute-start | bytes 1179656 | tf_op jit(solution)/shard_map/sum_core/ppermute | solution.py:481
  43.7 25.5 %all-to-all-start = ((f32[16,48,128]{2,1,0:T(8,128)}), f32[16,48,128]{2,1,0:T(8,128)S(1)}, u32[]{:S(2)}, u32[]{:S(2)}) async-start(f32[16,48,128]{2,1,0:T(8,128)} %bitcast.17), calls=%async_computation | async-start | bytes 786432 | tf_op jit(solution)/shard_map/sum_chips/all_to_all | solution.py:484
  85.5 3.7 %collective-permute-start.11 = (s16[1024,128]{1,0:T(8,128)(2,1)S(1)}, s16[1024,128]{1,0:T(8,128)(2,1)S(1)}, u32[]{:S(2)}, u32[]{:S(2)}) collective-permute-start(s16[1024,128]{1,0:T(8,128)(2,1)S(1)} %bitcast.14), channel_id=1, source_target_pairs={{0,8},{8,0},{1,9},{9,1},{2,10},{10,2},{3,11},{11,3},{4,12},{12,4},... | collective-permute-start | bytes 786440 | tf_op jit(solution)/shard_map/spread_core/ppermute | solution.py:490
